TPU v7x, 256 devices: a whole 4x4x8 slice. The times are simulated.
256 devices in a mesh: seq: 32 (over x, z_hi, core), basis: 8 (over z_lo, y).
Axes of the slice: x: 4, y: 4, z: 8 (z_hi: 4, z_lo: 2; z = z_hi * 2 + z_lo), core: 2. Of those that a mesh axis runs over, the one named last changes fastest.
Arguments:
- activations: bfloat16 [192, 128, 4096], P('seq'), may hold values from -6 to 6
- gradients: bfloat16 [192, 128, 4096], P('seq'), may hold values from -6 to 6
- act_basis: bfloat16 [4096, 4096], P('basis', 'seq'), may hold values from -0.09375 to 0.09375
- grad_basis: bfloat16 [4096, 4096], P('basis', 'seq'), may hold values from -0.09375 to 0.09375
Outputs:
- correction: float32 [4096, 4096], P('seq', 'basis')
All inputs are finite; a program needn't handle non-finite values.
Results may differ from a plain program's by a relative error of at most 0.00078.
Values may be sent and summed in bfloat16 or wider, within the bound.
No kernel may reach another device: no remote copies, remote signals or barrier semaphores. Data moves between devices by JAX's collectives and lax.ppermute only.
A program may use at most 128 MiB of HBM per device.

v0:
```python
import jax
import jax.numpy as jnp
from jax import lax
from jax.sharding import PartitionSpec as P


def rotate_add(inputs, portion):
    return lax.dot_general(
        inputs, portion, (((1,), (1,)), ((), ())), preferred_element_type=jnp.float32
    )


def squared_block(act_block, rotated_grad):
    seq_count = act_block.shape[0]
    width_in = act_block.shape[2]
    width_out = rotated_grad.shape[2]

    def per_pair(pair_index, running):
        left = lax.dynamic_slice_in_dim(act_block, pair_index * 2, 2, 0)
        right = lax.dynamic_slice_in_dim(rotated_grad, pair_index * 2, 2, 0)
        product = lax.dot_general(
            left, right, (((1,), (1,)), ((0,), (0,))), preferred_element_type=jnp.float32
        )
        return running + jnp.sum(product * product, axis=0)

    return lax.fori_loop(0, seq_count // 2, per_pair, jnp.zeros((width_in, width_out), jnp.float32))


def per_device(activations, gradients, act_basis, grad_basis):
    seq_count, seq_len, width = activations.shape
    flat_act = activations.reshape(seq_count * seq_len, width)
    flat_grad = gradients.reshape(seq_count * seq_len, width)
    act_sum = rotate_add(flat_act, lax.all_gather(act_basis, "seq", axis=1, tiled=True))
    grad_sum = rotate_add(flat_grad, lax.all_gather(grad_basis, "seq", axis=1, tiled=True))
    rotated_act = act_sum.astype(jnp.bfloat16).reshape(seq_count, seq_len, -1)
    rotated_grad = grad_sum.astype(jnp.bfloat16).reshape(seq_count, seq_len, -1)
    terms = squared_block(lax.all_gather(rotated_act, "basis", axis=2, tiled=True), rotated_grad)
    summed = lax.psum_scatter(terms, "seq", scatter_dimension=0, tiled=True)
    all_seqs = seq_count * lax.axis_size("seq")
    return summed / jnp.float32(all_seqs * seq_len)


def solution(mesh):
    placed = (P("seq", None, None), P("seq", None, None), P("basis", "seq"), P("basis", "seq"))
    return jax.shard_map(
        per_device, mesh=mesh, in_specs=placed, out_specs=P("seq", "basis"), check_vma=False
    )
```

profile of v0, /device:TPU:1, one launch (start us, length us, event | category | flops | bytes accessed | tf_op | source)
XLA Modules:
  0.0 399.6 jit_solution(1922507375022843597)
XLA Ops:
  6.5 0.0 all-gather.4.cloned.1.call-start
  6.5 0.7 all-gather.4.cloned.1.call-update
  7.3 0.0 all-gather.8.cloned.1.call-start
  7.3 0.7 all-gather.8.cloned.1.call-update
  8.0 0.0 all-gather.6.cloned.1.call-start
  8.1 70.8 %all-gather.4.cloned.1.call-done = bf16[512,4096]{1,0:T(8,128)(2,1)} async-done(((bf16[512,128]{1,0:T(8,128)(2,1)}), bf16[512,4096]{1,0:T(8,128)(2,1)}) %all-gather.4.cloned.1.call-update) | async-done | bytes 4194320 | tf_op jit(solution)/shard_map/all_gather | solution.py:33
  78.9 7.4 %convolution_convert_fusion.1 = bf16[768,512]{1,0:T(8,128)(2,1)S(1)} fusion(bf16[768,4096]{1,0:T(8,128)(2,1)} %bitcast.10, bf16[512,4096]{1,0:T(8,128)(2,1)} %all-gather.4.cloned.1.call-done), kind=kOutput, calls=%fused_computation.6 | convolution fusion | flops 3221618688 | bytes 11272192 | tf_op jit(solution)/shard_map/dot_general | solution.py:8
  86.3 1.2 copy.5
  87.6 0.0 all-gather.6.cloned.1.call-update
  87.6 0.2 reduce-scatter.2.cloned.1.call-start
  87.8 55.7 %all-gather.8.cloned.1.call-done = bf16[512,4096]{1,0:T(8,128)(2,1)} async-done(((bf16[512,128]{1,0:T(8,128)(2,1)}), bf16[512,4096]{1,0:T(8,128)(2,1)}) %all-gather.8.cloned.1.call-update) | async-done | bytes 4194320 | tf_op jit(solution)/shard_map/all_gather | solution.py:34
  143.5 7.4 %convolution_convert_fusion = bf16[768,512]{1,0:T(8,128)(2,1)S(1)} fusion(bf16[768,4096]{1,0:T(8,128)(2,1)} %bitcast.11, bf16[512,4096]{1,0:T(8,128)(2,1)} %all-gather.8.cloned.1.call-done), kind=kOutput, calls=%fused_computation.5 | convolution fusion | flops 3221618688 | bytes 11272192 | tf_op jit(solution)/shard_map/dot_general | solution.py:8
  151.0 66.1 %all-gather.6.cloned.1.call-done = bf16[6,128,4096]{1,2,0:T(8,128)(2,1)} async-done(((bf16[6,128,512]{1,2,0:T(8,128)(2,1)}), bf16[6,128,4096]{1,2,0:T(8,128)(2,1)}) %all-gather.6.cloned.1.call-update) | async-done | bytes 6291472 | tf_op jit(solution)/shard_map/all_gather | solution.py:37
  217.1 54.6 %while.14 = (s32[]{:T(128)}, f32[4096,512]{1,0:T(8,128)}, bf16[6,128,4096]{1,2,0:T(8,128)(2,1)}, bf16[6,128,512]{2,1,0:T(8,128)(2,1)S(1)}, s32[]{:T(128)}, /*index=5*/s32[]{:T(128)}, s32[]{:T(128)}, s32[]{:T(128)}) while((s32[]{:T(128)}, f32[4096,512]{1,0:T(8,128)}, bf16[6,128,4096]{1,2,0:T(8,128)(2,1)}, ...), condition=%wide.region_2.0_spmd.clone, body=%wide.region_0.0_spmd.clone.sunk | while | flops 1084227584 | bytes 35914900 | solution.py:26
  217.1 7.9 %multiply_reduce_fusion.2 = f32[4096,512]{1,0:T(8,128)} fusion(bf16[6,128,4096]{1,2,0:T(8,128)(2,1)} %get-tuple-element.151, s32[]{:T(128)S(6)} %select_n.10, bf16[6,128,512]{2,1,0:T(8,128)(2,1)S(1)} %get-tuple-element.152), kind=kOutput, calls=%fused_computation.clone.1 | convolution fusion | flops 1080033280 | bytes 10748928 | tf_op jit(solution)/shard_map/while/body/eval_jaxpr/dot_general | solution.py:21
  225.0 8.7 %select_add_fusion.2 = f32[4096,512]{1,0:T(8,128)} fusion(f32[4096,512]{1,0:T(8,128)} %multiply_reduce_fusion.2, f32[4096,512]{1,0:T(8,128)} %get-tuple-element.142, pred[]{:T(512)S(6)} %compare.3), kind=kLoop, calls=%fused_computation.1.clone.1 | loop fusion | flops 4194304 | bytes 25165824 | tf_op jit(solution)/shard_map/while/body/eval_jaxpr/add | solution.py:24
  233.7 7.9 %multiply_reduce_fusion.2 = f32[4096,512]{1,0:T(8,128)} fusion(bf16[6,128,4096]{1,2,0:T(8,128)(2,1)} %get-tuple-element.151, s32[]{:T(128)S(6)} %select_n.10, bf16[6,128,512]{2,1,0:T(8,128)(2,1)S(1)} %get-tuple-element.152), kind=kOutput, calls=%fused_computation.clone.1 | convolution fusion | flops 1080033280 | bytes 10748928 | tf_op jit(solution)/shard_map/while/body/eval_jaxpr/dot_general | solution.py:21
  241.6 11.1 %select_add_fusion.2 = f32[4096,512]{1,0:T(8,128)} fusion(f32[4096,512]{1,0:T(8,128)} %multiply_reduce_fusion.2, f32[4096,512]{1,0:T(8,128)} %get-tuple-element.142, pred[]{:T(512)S(6)} %compare.3), kind=kLoop, calls=%fused_computation.1.clone.1 | loop fusion | flops 4194304 | bytes 25165824 | tf_op jit(solution)/shard_map/while/body/eval_jaxpr/add | solution.py:24
  252.7 7.9 %multiply_reduce_fusion.2 = f32[4096,512]{1,0:T(8,128)} fusion(bf16[6,128,4096]{1,2,0:T(8,128)(2,1)} %get-tuple-element.151, s32[]{:T(128)S(6)} %select_n.10, bf16[6,128,512]{2,1,0:T(8,128)(2,1)S(1)} %get-tuple-element.152), kind=kOutput, calls=%fused_computation.clone.1 | convolution fusion | flops 1080033280 | bytes 10748928 | tf_op jit(solution)/shard_map/while/body/eval_jaxpr/dot_general | solution.py:21
  260.6 11.1 %select_add_fusion.2 = f32[4096,512]{1,0:T(8,128)} fusion(f32[4096,512]{1,0:T(8,128)} %multiply_reduce_fusion.2, f32[4096,512]{1,0:T(8,128)} %get-tuple-element.142, pred[]{:T(512)S(6)} %compare.3), kind=kLoop, calls=%fused_computation.1.clone.1 | loop fusion | flops 4194304 | bytes 25165824 | tf_op jit(solution)/shard_map/while/body/eval_jaxpr/add | solution.py:24
  271.7 0.0 reduce-scatter.2.cloned.1.call-update
  271.7 119.7 %reduce-scatter.2.cloned.1.call-done = f32[128,512]{1,0:T(8,128)} async-done(((f32[4096,512]{1,0:T(8,128)}), f32[128,512]{1,0:T(8,128)}) %reduce-scatter.2.cloned.1.call-update) | async-done | bytes 262160 | tf_op jit(solution)/shard_map/reduce_scatter | solution.py:38
  391.4 1.7 broadcast_multiply_fusion
  (1 shorter events, 0.0 us)
Async XLA Ops:
  6.5 72.4 %all-gather.4.cloned.1.call-start = ((), (), s32[]{:S(2)}) async-start(), calls=%async_computation.1 | async-start | bytes 4325376 | tf_op jit(solution)/shard_map/all_gather | solution.py:33
  7.3 136.3 %all-gather.8.cloned.1.call-start = ((), (), s32[]{:S(2)}) async-start(), calls=%async_computation.3 | async-start | bytes 4325376 | tf_op jit(solution)/shard_map/all_gather | solution.py:34
  8.0 209.1 %all-gather.6.cloned.1.call-start = ((), (), s32[]{:S(2)}) async-start(), calls=%async_computation.2 | async-start | bytes 7077888 | tf_op jit(solution)/shard_map/all_gather | solution.py:37
  87.6 303.8 %reduce-scatter.2.cloned.1.call-start = ((), (), s32[]{:S(2)}) async-start(), calls=%async_computation.4 | async-start | bytes 8650752 | tf_op jit(solution)/shard_map/reduce_scatter | solution.py:38
Sparse Core Ops, SparseCore 0:
  9.8 69.0 all-gather.3
  81.4 62.1 all-gather.7
  145.3 71.7 all-gather.5
  271.8 119.5 reduce-scatter.1
where the time goes:
time: 400 us
  waiting for transfers between devices  314 us (78%)
  matrix products  38.5 us (10%)
  other arithmetic  32.6 us (8%)
  between operations  13.1 us (3%)
    reduce_scatter x1, waiting for transfers between devices, per_device(): summed = lax.psum_scatter(terms, 'seq', scatter_dimension=0, tiled=True)  120 us
    all_gather x1, waiting for transfers between devices, per_device(): lax.all_gather(act_basis, 'seq', axis=1, tiled=True)  70.8 us
    all_gather x1, waiting for transfers between devices, per_device(): lax.all_gather(rotated_act, 'basis', axis=2, tiled=True)  66.1 us
    all_gather x1, waiting for transfers between devices, per_device(): lax.all_gather(grad_basis, 'seq', axis=1, tiled=True)  55.7 us
    add x3, other arithmetic, per_pair(): return running + jnp.sum(product * product, axis=0)  31 us
    dot_general x3, matrix products, per_pair(): lax.dot_general(left, right, (((1,), (1,)), ((0,), (0,))), preferred_elem...  23.6 us
    dot_general x2, matrix products, rotate_add(): lax.dot_general(inputs, portion, (((1,), (1,)), ((), ())), preferred_elem...  14.9 us
  transfers between devices with their start and end apart: 4, of which 4 were waited for; matrix products, arithmetic and copies ran while one was open for 4% of the time, Pallas kernels for 0%

commit v1 on v0

v1 whole, which is shorter than its diff:
```python
import functools

import jax
import jax.numpy as jnp
from jax import lax
from jax.experimental import pallas as pl
from jax.experimental.pallas import tpu as pltpu
from jax.sharding import PartitionSpec as P

NX, NZ, NC, NL, NY = 4, 4, 2, 2, 4
NT = (((1,), (1,)), ((), ()))
VMEM = 48 << 20
BIAS = 14.0


def seq_perm(value, move):
    pairs = []
    for i in range(NX * NZ * NC):
        x, zh, c = move(i // (NZ * NC), i // NC % NZ, i % NC)
        pairs.append((i, ((x % NX) * NZ + zh % NZ) * NC + c % NC))
    return lax.ppermute(value, "seq", pairs)


def basis_perm(value, move):
    pairs = []
    for j in range(NL * NY):
        zl, y = move(j // NY, j % NY)
        pairs.append((j, (zl % NL) * NY + y % NY))
    return lax.ppermute(value, "basis", pairs)


def swap_core(value):
    return seq_perm(value, lambda x, zh, c: (x, zh, c + 1))


def from_x(value, d):
    return seq_perm(value, lambda x, zh, c: (x - d, zh, c))


def from_zh(value, d):
    return seq_perm(value, lambda x, zh, c: (x, zh - d, c))


def from_y(value, d):
    return basis_perm(value, lambda zl, y: (zl, y - d))


def swap_zl(value):
    return basis_perm(value, lambda zl, y: (zl + 1, y))


def to_owner(value):
    pairs = []
    for i in range(NX * NZ * NC):
        for j in range(NL * NY):
            xt, zt, c, zl, y = i // (NZ * NC), i // NC % NZ, i % NC, j // NY, j % NY
            x, zh, core = 2 * ((xt // 2) ^ zl) + y // 2, 2 * (y % 2) + c, xt % 2
            seq, basis = (x * NZ + zh) * NC + core, zl * NY + (y + zt) % NY
            pairs.append((i * NL * NY + j, seq * NL * NY + basis))
    return lax.ppermute(value, ("seq", "basis"), pairs)


def rotate_kernel(flip, tiles, places, own, sibling, p0, p1, p2, p3, out, rows_of):
    step = pl.program_id(0)
    width = p0.shape[2]

    @pl.when(step == 0)
    def _():
        for d, piece in enumerate((p0, p1, p2, p3)):
            for q in range(NZ):
                at = pl.multiple_of(places[d * NZ + q] * width, width)
                rows_of[:, pl.ds(at, width)] = piece[q]

    tile = own.shape[0]
    for half, block in enumerate((own, sibling)):

        @pl.when(step // tiles == half)
        def _():
            total = lax.dot_general(block[...], rows_of[...], NT, preferred_element_type=jnp.float32)
            slot = (places[NX * NZ] ^ half) * tiles + step - half * tiles
            at = pl.multiple_of(slot * tile, tile)
            if flip:
                out[:, pl.ds(at, tile)] = total.T.astype(jnp.bfloat16)
            else:
                out[pl.ds(at, tile), :] = total.astype(jnp.bfloat16)


def rotate(places, own, sibling, pieces, flip):
    tokens, width = own.shape
    rows = pieces[0].shape[1]
    tiles = 3
    shape = (rows, 2 * tokens) if flip else (2 * tokens, rows)
    whole = pl.BlockSpec(pieces[0].shape, lambda s, places: (0, 0, 0))
    return pl.pallas_call(
        functools.partial(rotate_kernel, flip, tiles),
        out_shape=jax.ShapeDtypeStruct(shape, jnp.bfloat16),
        grid_spec=pltpu.PrefetchScalarGridSpec(
            num_scalar_prefetch=1,
            grid=(2 * tiles,),
            in_specs=[
                pl.BlockSpec((tokens // tiles, width), lambda s, places: (jnp.minimum(s, tiles - 1), 0)),
                pl.BlockSpec((tokens // tiles, width), lambda s, places: (jnp.maximum(s - tiles, 0), 0)),
            ]
            + [whole] * 4,
            out_specs=pl.BlockSpec(shape, lambda s, places: (0, 0)),
            scratch_shapes=[pltpu.VMEM((rows, width), jnp.bfloat16)],
        ),
        compiler_params=pltpu.CompilerParams(vmem_limit_bytes=VMEM),
        cost_estimate=pl.CostEstimate(
            flops=4 * tokens * rows * width, bytes_accessed=4 * tokens * width, transcendentals=0
        ),
    )(places, own, sibling, *pieces)


def product_kernel(seq_len, places, left0, left1, *rest):
    grads, out, left = rest[:8], rest[8], rest[9]
    step = pl.program_id(0)
    half = left0.shape[0]
    rows = 2 * half // NX
    width = grads[0].shape[1]

    @pl.when(step == 0)
    def _():
        left[:half, :] = left0[...]
        left[half:, :] = left1[...]

    piece = left[pl.ds(pl.multiple_of(places[step] * rows, rows), rows), :]
    top = jnp.zeros((1, 1), jnp.float32)
    for g in range(8):
        total = None
        for s in range(piece.shape[1] // seq_len):
            tokens = slice(s * seq_len, (s + 1) * seq_len)
            product = jnp.dot(piece[:, tokens], grads[g][tokens, :], preferred_element_type=jnp.float32)
            total = product * product if total is None else total + product * product
        row = pl.multiple_of(places[4 + g // 2] * rows, rows)
        column = pl.multiple_of((places[8] ^ (g % 2)) * width, width)
        out[0, pl.ds(row, rows), pl.ds(column, width)] = total
        top = jnp.maximum(top, jnp.max(jnp.max(total, axis=0, keepdims=True), axis=1, keepdims=True))
    power = jnp.clip(jnp.ceil(jnp.log2(top)), -100.0, 130.0)
    out[0, 4 * rows :, :] = jnp.broadcast_to(power, (16, 2 * width))


def products(places, left, grads, seq_len):
    half, tokens = left[0].shape
    width = grads[0].shape[1]
    shape = (NX, 2 * half + 16, 2 * width)
    return pl.pallas_call(
        functools.partial(product_kernel, seq_len),
        out_shape=jax.ShapeDtypeStruct(shape, jnp.float32),
        grid_spec=pltpu.PrefetchScalarGridSpec(
            num_scalar_prefetch=1,
            grid=(NX,),
            in_specs=[pl.BlockSpec((half, tokens), lambda s, places: (0, 0))] * 2
            + [pl.BlockSpec((tokens, width), lambda s, places: (0, 0))] * 8,
            out_specs=pl.BlockSpec((1,) + shape[1:], lambda s, places: (s, 0, 0)),
            scratch_shapes=[pltpu.VMEM((2 * half, tokens), jnp.bfloat16)],
        ),
        compiler_params=pltpu.CompilerParams(vmem_limit_bytes=VMEM),
        cost_estimate=pl.CostEstimate(
            flops=16 * half * tokens * width, bytes_accessed=20 * tokens * width, transcendentals=0
        ),
    )(places, *left, *grads)


def shrink(block, power):
    return block * jnp.exp2(BIAS - power)


def grow(sent):
    power = sent[-1, 0].astype(jnp.float32)
    return sent[:-16].astype(jnp.float32) * jnp.exp2(power - BIAS)


def gather_rows(shard):
    column = jnp.stack([shard] + [from_zh(shard, d) for d in range(1, NZ)])
    return [column] + [from_x(column, d) for d in range(1, NX)]


def per_device(activations, gradients, act_basis, grad_basis):
    seq_count, seq_len, width = activations.shape
    seq, basis = lax.axis_index("seq"), lax.axis_index("basis")
    x, zh, core = seq // (NZ * NC), seq // NC % NZ, seq % NC
    act = activations.reshape(seq_count * seq_len, width)
    grad = gradients.reshape(seq_count * seq_len, width)

    half = act_basis.shape[0] // 2

    def mine(shard, which):
        return lax.dynamic_slice_in_dim(shard, which * half, half, 0)

    kept = jnp.concatenate([mine(grad_basis, core), mine(act_basis, core)])
    got = swap_core(jnp.concatenate([mine(grad_basis, 1 - core), mine(act_basis, 1 - core)]))
    pair = jnp.where(core == 0, jnp.concatenate([kept, got], 1), jnp.concatenate([got, kept], 1))
    grad_pieces = gather_rows(pair[:half])
    act_pieces = gather_rows(pair[half:])
    grad_sib, act_sib = swap_core(grad), swap_core(act)

    steps = jnp.arange(4)
    feature_of = ((x + steps[:, None]) % NX) * NZ + (zh + steps[None, :]) % NZ
    places = jnp.concatenate([feature_of.reshape(-1), core[None]]).astype(jnp.int32)
    rotated_grad = rotate(places, grad, grad_sib, grad_pieces, False)
    rotated_act = rotate(places, act, act_sib, act_pieces, True)

    grads = [rotated_grad] + [from_y(rotated_grad, d) for d in range(1, NY)]
    both = []
    for block in grads:
        both += [block, swap_core(block)]
    left = [rotated_act, swap_zl(rotated_act)]

    places = jnp.concatenate([(x + steps) % NX, (steps - zh) % NZ, core[None]]).astype(jnp.int32)
    terms = products(places, left, both, seq_len)

    def packed(d):
        term = terms[d]
        power = term[-1, 0]
        inside = lax.broadcasted_iota(jnp.int32, term.shape, 0) < term.shape[0] - 16
        return jnp.where(inside, shrink(term, power), power).astype(jnp.float16)

    total = terms[0, :-16]
    for d in range(1, NX):
        total = total + grow(from_x(packed(d), -d))
    rows = total.shape[0] // NZ
    power = jnp.clip(jnp.ceil(jnp.log2(jnp.max(total))), -100.0, 130.0)
    final = total[:rows]
    for d in range(1, NZ):
        block = shrink(total[d * rows : (d + 1) * rows], power)
        sent = jnp.concatenate([block, jnp.full((16, block.shape[1]), power)]).astype(jnp.float16)
        final = final + grow(from_zh(sent, -d))
    all_seqs = seq_count * NX * NZ * NC
    return to_owner(final / jnp.float32(all_seqs * seq_len))


def solution(mesh):
    placed = (P("seq", None, None), P("seq", None, None), P("basis", "seq"), P("basis", "seq"))
    return jax.shard_map(
        per_device, mesh=mesh, in_specs=placed, out_specs=P("seq", "basis"), check_vma=False
    )
```

time: 400 us -> 232 us (0.58)
  the two profiles are of different devices: /device:TPU:1 before, /device:TPU:33 now
where the time goes in v1:
time: 232 us; the launch traced here: 231 us
  waiting for transfers between devices  108 us (47%)
  starting transfers between devices  68.3 us (29%)
  Pallas kernels  30.1 us (13%)
  local copies, waits for them, and re-layouts  10.6 us (5%)
  other arithmetic  7.14 us (3%)
  between operations  6.98 us (3%)
    ppermute x25, waiting for transfers between devices, seq_perm(): return lax.ppermute(value, 'seq', pairs)  72.2 us
    ppermute x25, starting transfers between devices, seq_perm(): return lax.ppermute(value, 'seq', pairs)  61 us
    ppermute x1, waiting for transfers between devices, to_owner(): return lax.ppermute(value, ('seq', 'basis'), pairs)  27.5 us
    pallas_call x2, Pallas kernels, rotate(): pl.pallas_call(functools.partial(rotate_kernel, flip, tiles), out_shape=j...  19.2 us
    pallas_call x1, Pallas kernels, products(): pl.pallas_call(functools.partial(product_kernel, seq_len), out_shape=jax....  10.8 us
    ppermute x4, waiting for transfers between devices, basis_perm(): return lax.ppermute(value, 'basis', pairs)  8.58 us
    ppermute x4, starting transfers between devices, basis_perm(): return lax.ppermute(value, 'basis', pairs)  5.39 us
  transfers between devices with their start and end apart: 30, of which 15 were waited for; matrix products, arithmetic and copies ran while one was open for 2% of the time, Pallas kernels for 8%

profile of v1, /device:TPU:33, one launch (start us, length us, event | category | flops | bytes accessed | tf_op | source)
XLA Modules:
  0.0 231.5 jit_solution(16705068408994630472)
XLA Ops:
  0.0 0.7 collective-permute-start.9
  0.7 1.0 constant_dynamic-slice_fusion.2
  1.7 0.6 collective-permute-start.1
  2.2 8.6 %collective-permute-done.1 = bf16[512,128]{1,0:T(8,128)(2,1)S(1)} collective-permute-done((bf16[512,128]{1,0:T(8,128)(2,1)S(1)}, bf16[512,128]{1,0:T(8,128)(2,1)S(1)}, u32[]{:S(2)}, u32[]{:S(2)}) %collective-permute-start.1) | collective-permute-done | bytes 131104 | tf_op jit(solution)/shard_map/ppermute | solution.py:21
  10.8 0.1 maximum_select_fusion
  11.0 3.1 %collective-permute-start.12 = (bf16[256,256]{1,0:T(8,128)(2,1)S(1)}, bf16[256,256]{1,0:T(8,128)(2,1)S(1)}, u32[]{:S(2)}, u32[]{:S(2)}) collective-permute-start(bf16[256,256]{1,0:T(8,128)(2,1)S(1)} %get-tuple-element.18), channel_id=1, source_target_pairs={{0,16},{8,24},{16,32},{24,40},{32,48},{40,56},{48,0},{56,8},{64,80... | collective-permute-start | bytes 393224 | tf_op jit(solution)/shard_map/ppermute | solution.py:21
  14.0 4.2 %collective-permute-start.11 = (bf16[256,256]{1,0:T(8,128)(2,1)S(1)}, bf16[256,256]{1,0:T(8,128)(2,1)S(1)}, u32[]{:S(2)}, u32[]{:S(2)}) collective-permute-start(bf16[256,256]{1,0:T(8,128)(2,1)S(1)} %get-tuple-element.18), channel_id=1, source_target_pairs={{0,32},{8,40},{16,48},{24,56},{32,0},{40,8},{48,16},{56,24},{64,96... | collective-permute-start | bytes 393224 | tf_op jit(solution)/shard_map/ppermute | solution.py:21
  18.3 2.4 %collective-permute-start.10 = (bf16[256,256]{1,0:T(8,128)(2,1)S(1)}, bf16[256,256]{1,0:T(8,128)(2,1)S(1)}, u32[]{:S(2)}, u32[]{:S(2)}) collective-permute-start(bf16[256,256]{1,0:T(8,128)(2,1)S(1)} %get-tuple-element.18), channel_id=1, source_target_pairs={{0,48},{8,56},{16,0},{24,8},{32,16},{40,24},{48,32},{56,40},{64,11... | collective-permute-start | bytes 393224 | tf_op jit(solution)/shard_map/ppermute | solution.py:21
  20.6 2.3 collective-permute-done.12
  22.9 0.9 collective-permute-start.4
  23.8 4.0 %collective-permute-done.10 = bf16[256,256]{1,0:T(8,128)(2,1)S(1)} collective-permute-done((bf16[256,256]{1,0:T(8,128)(2,1)S(1)}, bf16[256,256]{1,0:T(8,128)(2,1)S(1)}, u32[]{:S(2)}, u32[]{:S(2)}) %collective-permute-start.10) | collective-permute-done | bytes 131104 | tf_op jit(solution)/shard_map/ppermute | solution.py:21
  27.9 2.6 %collective-permute-start.13 = (bf16[4,256,256]{2,1,0:T(8,128)(2,1)S(1)}, bf16[4,256,256]{2,1,0:T(8,128)(2,1)S(1)}, u32[]{:S(2)}, u32[]{:S(2)}) collective-permute-start(bf16[4,256,256]{2,1,0:T(8,128)(2,1)S(1)} %pad_maximum_fusion.1.p0), channel_id=1, source_target_pairs={{0,192},{8,200},{16,208},{24,216},{32,224},{40,232},{48,240},{56,2... | collective-permute-start | bytes 1572872 | tf_op jit(solution)/shard_map/ppermute | solution.py:21
  30.4 0.5 collective-permute-start.14
  31.0 2.5 %collective-permute-done.4 = bf16[256,256]{1,0:T(8,128)(2,1)S(1)} collective-permute-done((bf16[256,256]{1,0:T(8,128)(2,1)S(1)}, bf16[256,256]{1,0:T(8,128)(2,1)S(1)}, u32[]{:S(2)}, u32[]{:S(2)}) %collective-permute-start.4) | collective-permute-done | bytes 131104 | tf_op jit(solution)/shard_map/ppermute | solution.py:21
  33.5 4.9 %collective-permute-start.3 = (bf16[256,256]{1,0:T(8,128)(2,1)S(1)}, bf16[256,256]{1,0:T(8,128)(2,1)S(1)}, u32[]{:S(2)}, u32[]{:S(2)}) collective-permute-start(bf16[256,256]{1,0:T(8,128)(2,1)S(1)} %get-tuple-element.19), channel_id=1, source_target_pairs={{0,32},{8,40},{16,48},{24,56},{32,0},{40,8},{48,16},{56,24},{64,96... | collective-permute-start | bytes 393224 | tf_op jit(solution)/shard_map/ppermute | solution.py:21
  38.4 2.9 %collective-permute-done.3 = bf16[256,256]{1,0:T(8,128)(2,1)S(1)} collective-permute-done((bf16[256,256]{1,0:T(8,128)(2,1)S(1)}, bf16[256,256]{1,0:T(8,128)(2,1)S(1)}, u32[]{:S(2)}, u32[]{:S(2)}) %collective-permute-start.3) | collective-permute-done | bytes 131104 | tf_op jit(solution)/shard_map/ppermute | solution.py:21
  41.3 1.4 collective-permute-start.2
  42.7 4.3 %collective-permute-done.2 = bf16[256,256]{1,0:T(8,128)(2,1)S(1)} collective-permute-done((bf16[256,256]{1,0:T(8,128)(2,1)S(1)}, bf16[256,256]{1,0:T(8,128)(2,1)S(1)}, u32[]{:S(2)}, u32[]{:S(2)}) %collective-permute-start.2) | collective-permute-done | bytes 131104 | tf_op jit(solution)/shard_map/ppermute | solution.py:21
  47.0 1.5 collective-permute-start.15
  48.6 1.3 collective-permute-start.5
  50.0 1.5 collective-permute-start.6
  51.7 4.8 %collective-permute-done.15.p3 = bf16[4,256,256]{2,1,0:T(8,128)(2,1)} collective-permute-done((bf16[4,256,256]{2,1,0:T(8,128)(2,1)S(1)}, bf16[4,256,256]{2,1,0:T(8,128)(2,1)}, u32[]{:S(2)}, u32[]{:S(2)}) %collective-permute-start.15) | collective-permute-done | bytes 524320 | tf_op jit(solution)/shard_map/ppermute | solution.py:21
  56.5 0.7 collective-permute-start.7
  57.1 9.5 %shard_map.47.rest_0_ = bf16[1536,256]{1,0:T(8,128)(2,1)S(1)} custom-call(s32[17]{0:T(128)S(1)} %pad_add_fusion.1.places, bf16[768,4096]{1,0:T(8,128)(2,1)} %bitcast.44, bf16[768,4096]{1,0:T(8,128)(2,1)} %collective-permute-done.9.sibling, bf16[4,256,256]{2,1,0:T(8,128)(2,1)S(1)} %pad_maximum_fusion.1.p0, ...), custom_call_target="tpu_custom_call" | custom-call | flops 3221225472 | bytes 12582912 | tf_op jit(solution)/shard_map/pallas_call | solution.py:94
  66.7 3.0 %collective-permute-start.17 = (bf16[1536,256]{1,0:T(8,128)(2,1)S(1)}, bf16[1536,256]{1,0:T(8,128)(2,1)S(1)}, u32[]{:S(2)}, u32[]{:S(2)}) collective-permute-start(bf16[1536,256]{1,0:T(8,128)(2,1)S(1)} %shard_map.47.rest_0_), channel_id=1, source_target_pairs={{0,3},{1,0},{2,1},{3,2},{4,7},{5,4},{6,5},{7,6},{8,11},{9,8},{10,9... | collective-permute-start | bytes 2359304 | tf_op jit(solution)/shard_map/ppermute | solution.py:29
  69.7 0.4 collective-permute-start.19
  70.0 0.7 collective-permute-start.21
  70.7 7.6 %collective-permute-done.7.p3 = bf16[4,256,256]{2,1,0:T(8,128)(2,1)S(1)} collective-permute-done((bf16[4,256,256]{2,1,0:T(8,128)(2,1)S(1)}, bf16[4,256,256]{2,1,0:T(8,128)(2,1)S(1)}, u32[]{:S(2)}, u32[]{:S(2)}) %collective-permute-start.7) | collective-permute-done | bytes 524320 | tf_op jit(solution)/shard_map/ppermute | solution.py:21
  78.3 16.1 %collective-permute-start.16 = (bf16[1536,256]{1,0:T(8,128)(2,1)S(1)}, bf16[1536,256]{1,0:T(8,128)(2,1)S(1)}, u32[]{:S(2)}, u32[]{:S(2)}) collective-permute-start(bf16[1536,256]{1,0:T(8,128)(2,1)S(1)} %shard_map.47.rest_0_), channel_id=1, source_target_pairs={{0,8},{8,0},{16,24},{24,16},{32,40},{40,32},{48,56},{56,48},{64,72... | collective-permute-start | bytes 2359304 | tf_op jit(solution)/shard_map/ppermute | solution.py:21
  94.4 9.7 %shard_map.46.left0 = bf16[256,1536]{1,0:T(8,128)(2,1)S(1)} custom-call(s32[17]{0:T(128)S(1)} %pad_add_fusion.1.places, bf16[768,4096]{1,0:T(8,128)(2,1)} %bitcast.46, bf16[768,4096]{1,0:T(8,128)(2,1)} %collective-permute-done.sibling, bf16[4,256,256]{2,1,0:T(8,128)(2,1)S(1)} %pad_maximum_fusion.p0, bf16[4,256,256]{2,1,0:T(8,128)(2,1)S(1)} %collective-permute-done.5.p1, ...), custom_call_target="tpu_custom_call" | custom-call | flops 3221225472 | bytes 12582912 | tf_op jit(solution)/shard_map/pallas_call | solution.py:94
  104.1 1.4 collective-permute-start.8
  105.5 5.2 %collective-permute-start.18 = (bf16[1536,256]{1,0:T(8,128)(2,1)S(1)}, bf16[1536,256]{1,0:T(8,128)(2,1)S(1)}, u32[]{:S(2)}, u32[]{:S(2)}) collective-permute-start(bf16[1536,256]{1,0:T(8,128)(2,1)S(1)} %collective-permute-done.17.rest_2_), channel_id=1, source_target_pairs={{0,8},{8,0},{16,24},{24,16},{32,40},{40,32},{48,56},{56,48},{64,72... | collective-permute-start | bytes 2359304 | tf_op jit(solution)/shard_map/ppermute | solution.py:21
  110.7 4.0 %collective-permute-start.22 = (bf16[1536,256]{1,0:T(8,128)(2,1)S(1)}, bf16[1536,256]{1,0:T(8,128)(2,1)S(1)}, u32[]{:S(2)}, u32[]{:S(2)}) collective-permute-start(bf16[1536,256]{1,0:T(8,128)(2,1)S(1)} %collective-permute-done.21.rest_6_), channel_id=1, source_target_pairs={{0,8},{8,0},{16,24},{24,16},{32,40},{40,32},{48,56},{56,48},{64,72... | collective-permute-start | bytes 2359304 | tf_op jit(solution)/shard_map/ppermute | solution.py:21
  114.8 8.6 %collective-permute-done.8.left1 = bf16[256,1536]{1,0:T(8,128)(2,1)S(1)} collective-permute-done((bf16[256,1536]{1,0:T(8,128)(2,1)S(1)}, bf16[256,1536]{1,0:T(8,128)(2,1)S(1)}, u32[]{:S(2)}, u32[]{:S(2)}) %collective-permute-start.8) | collective-permute-done | bytes 786464 | tf_op jit(solution)/shard_map/ppermute | solution.py:29
  123.4 0.9 copy-done.1
  124.3 0.9 copy-done.2
  125.2 10.8 %shard_map.48 = f32[4,528,512]{2,1,0:T(8,128)} custom-call(s32[9]{0:T(128)S(1)} %pad_add_fusion.places, bf16[256,1536]{1,0:T(8,128)(2,1)S(1)} %shard_map.46.left0, bf16[256,1536]{1,0:T(8,128)(2,1)S(1)} %collective-permute-done.8.left1, bf16[1536,256]{1,0:T(8,128)(2,1)S(1)} %shard_map.47.rest_0_, bf16[1536,256]{1,0:T(8,128)(2,1)S(1)} %collective-permute-done.16.rest_1_, ...), custom_call_target="tpu_custom_call" | custom-call | flops 1610612736 | bytes 7864320 | tf_op jit(solution)/shard_map/pallas_call | solution.py:147
  136.0 2.2 slice_bitcast_fusion.2
  138.2 0.5 slice.104
  139.4 0.6 slice.108
  140.7 0.5 slice.112
  141.9 4.2 %select_convert_fusion.2 = (f16[528,512]{1,0:T(8,128)(2,1)S(1)}, f16[528,512]{1,0:T(8,128)(2,1)S(1)}, f16[528,512]{1,0:T(8,128)(2,1)S(1)}) fusion(f32[]{:T(128)} %bitcast.13, f32[]{:T(128)S(6)} %exp2.89, pred[528]{0:T(1024)(128)(4,1)S(1)} %iota_compare_fusion, f32[4,528,512]{2,1,0:T(8,128)} %shard_map.48, f32[]{:T(128)} %bitcast.16, f32[]{:T(128)S(6)} %exp2.94, ...), kind=kLoop, calls=%fused_computation.5 | loop fusion | flops 2433024 | bytes 4866600 | tf_op jit(solution)/shard_map/convert_element_type | solution.py:217
  146.1 3.1 %collective-permute-start.25 = (f16[528,512]{1,0:T(8,128)(2,1)S(1)}, f16[528,512]{1,0:T(8,128)(2,1)S(1)}, u32[]{:S(2)}, u32[]{:S(2)}) collective-permute-start(f16[528,512]{1,0:T(8,128)(2,1)S(1)} %get-tuple-element.9), channel_id=1, source_target_pairs={{0,192},{8,200},{16,208},{24,216},{32,224},{40,232},{48,240},{56,2... | collective-permute-start | bytes 1622024 | tf_op jit(solution)/shard_map/ppermute | solution.py:21
  149.1 1.1 collective-permute-start.24
  150.3 10.3 %collective-permute-done.25 = f16[528,512]{1,0:T(8,128)(2,1)S(1)} collective-permute-done((f16[528,512]{1,0:T(8,128)(2,1)S(1)}, f16[528,512]{1,0:T(8,128)(2,1)S(1)}, u32[]{:S(2)}, u32[]{:S(2)}) %collective-permute-start.25) | collective-permute-done | bytes 540704 | tf_op jit(solution)/shard_map/ppermute | solution.py:21
  160.5 0.5 slice.114
  161.8 1.9 collective-permute-done.24
  163.6 0.6 slice.110
  164.9 11.6 %collective-permute-done.23 = f16[528,512]{1,0:T(8,128)(2,1)S(1)} collective-permute-done((f16[528,512]{1,0:T(8,128)(2,1)S(1)}, f16[528,512]{1,0:T(8,128)(2,1)S(1)}, u32[]{:S(2)}, u32[]{:S(2)}) %collective-permute-start.23) | collective-permute-done | bytes 540704 | tf_op jit(solution)/shard_map/ppermute | solution.py:21
  176.4 0.5 slice.106
  177.6 2.3 fusion.12
  180.6 0.1 fusion.5
  180.7 2.2 collective-permute-start.28
  183.0 2.4 %collective-permute-start.27 = (f16[144,512]{1,0:T(8,128)(2,1)S(1)}, f16[144,512]{1,0:T(8,128)(2,1)S(1)}, u32[]{:S(2)}, u32[]{:S(2)}) collective-permute-start(f16[144,512]{1,0:T(8,128)(2,1)S(1)} %concatenate.34), channel_id=1, source_target_pairs={{0,32},{8,40},{16,48},{24,56},{32,0},{40,8},{48,16},{56,24},{64,96... | collective-permute-start | bytes 442376 | tf_op jit(solution)/shard_map/ppermute | solution.py:21
  185.4 0.6 collective-permute-start.26
  186.0 0.6 collective-permute-done.28
  186.6 0.5 slice.124
  187.9 11.0 %collective-permute-done.27 = f16[144,512]{1,0:T(8,128)(2,1)S(1)} collective-permute-done((f16[144,512]{1,0:T(8,128)(2,1)S(1)}, f16[144,512]{1,0:T(8,128)(2,1)S(1)}, u32[]{:S(2)}, u32[]{:S(2)}) %collective-permute-start.27) | collective-permute-done | bytes 147488 | tf_op jit(solution)/shard_map/ppermute | solution.py:21
  198.8 0.5 slice.121
  200.0 0.5 slice.118
  201.2 0.1 fusion.8
  201.3 1.9 collective-permute-start.29
  203.2 27.5 %collective-permute-done.29 = f32[128,512]{1,0:T(8,128)S(1)} collective-permute-done((f32[128,512]{1,0:T(8,128)S(1)}, f32[128,512]{1,0:T(8,128)S(1)}, u32[]{:S(2)}, u32[]{:S(2)}) %collective-permute-start.29) | collective-permute-done | bytes 262176 | tf_op jit(solution)/shard_map/ppermute | solution.py:60
  230.8 0.7 copy.6
  (36 shorter events, 0.7 us)
Async XLA Ops:
  0.0 57.1 %collective-permute-start.9 = (bf16[768,4096]{1,0:T(8,128)(2,1)}, bf16[768,4096]{1,0:T(8,128)(2,1)}, u32[]{:S(2)}, u32[]{:S(2)}) collective-permute-start(bf16[768,4096]{1,0:T(8,128)(2,1)} %bitcast.43), channel_id=1, source_target_pairs={{0,8},{8,0},{16,24},{24,16},{32,40},{40,32},{48,56},{56,48},{64,72... | collective-permute-start | bytes 18874376 | tf_op jit(solution)/shard_map/ppermute | solution.py:21
  0.7 93.7 %collective-permute-start = (bf16[768,4096]{1,0:T(8,128)(2,1)}, bf16[768,4096]{1,0:T(8,128)(2,1)}, u32[]{:S(2)}, u32[]{:S(2)}) collective-permute-start(bf16[768,4096]{1,0:T(8,128)(2,1)} %bitcast.45), channel_id=1, source_target_pairs={{0,8},{8,0},{16,24},{24,16},{32,40},{40,32},{48,56},{56,48},{64,72... | collective-permute-start | bytes 18874376 | tf_op jit(solution)/shard_map/ppermute | solution.py:21
  1.7 9.2 %collective-permute-start.1 = (bf16[512,128]{1,0:T(8,128)(2,1)S(1)}, bf16[512,128]{1,0:T(8,128)(2,1)S(1)}, u32[]{:S(2)}, u32[]{:S(2)}) collective-permute-start(bf16[512,128]{1,0:T(8,128)(2,1)S(1)} %pad_maximum_fusion.2), channel_id=1, source_target_pairs={{0,8},{8,0},{16,24},{24,16},{32,40},{40,32},{48,56},{56,48},{64,72... | collective-permute-start | bytes 393224 | tf_op jit(solution)/shard_map/ppermute | solution.py:21
  11.0 11.9 %collective-permute-start.12 = (bf16[256,256]{1,0:T(8,128)(2,1)S(1)}, bf16[256,256]{1,0:T(8,128)(2,1)S(1)}, u32[]{:S(2)}, u32[]{:S(2)}) collective-permute-start(bf16[256,256]{1,0:T(8,128)(2,1)S(1)} %get-tuple-element.18), channel_id=1, source_target_pairs={{0,16},{8,24},{16,32},{24,40},{32,48},{40,56},{48,0},{56,8},{64,80... | collective-permute-start | bytes 393224 | tf_op jit(solution)/shard_map/ppermute | solution.py:21
  14.0 9.8 %collective-permute-start.11 = (bf16[256,256]{1,0:T(8,128)(2,1)S(1)}, bf16[256,256]{1,0:T(8,128)(2,1)S(1)}, u32[]{:S(2)}, u32[]{:S(2)}) collective-permute-start(bf16[256,256]{1,0:T(8,128)(2,1)S(1)} %get-tuple-element.18), channel_id=1, source_target_pairs={{0,32},{8,40},{16,48},{24,56},{32,0},{40,8},{48,16},{56,24},{64,96... | collective-permute-start | bytes 393224 | tf_op jit(solution)/shard_map/ppermute | solution.py:21
  18.3 9.6 %collective-permute-start.10 = (bf16[256,256]{1,0:T(8,128)(2,1)S(1)}, bf16[256,256]{1,0:T(8,128)(2,1)S(1)}, u32[]{:S(2)}, u32[]{:S(2)}) collective-permute-start(bf16[256,256]{1,0:T(8,128)(2,1)S(1)} %get-tuple-element.18), channel_id=1, source_target_pairs={{0,48},{8,56},{16,0},{24,8},{32,16},{40,24},{48,32},{56,40},{64,11... | collective-permute-start | bytes 393224 | tf_op jit(solution)/shard_map/ppermute | solution.py:21
  22.9 10.6 %collective-permute-start.4 = (bf16[256,256]{1,0:T(8,128)(2,1)S(1)}, bf16[256,256]{1,0:T(8,128)(2,1)S(1)}, u32[]{:S(2)}, u32[]{:S(2)}) collective-permute-start(bf16[256,256]{1,0:T(8,128)(2,1)S(1)} %get-tuple-element.19), channel_id=1, source_target_pairs={{0,16},{8,24},{16,32},{24,40},{32,48},{40,56},{48,0},{56,8},{64,80... | collective-permute-start | bytes 393224 | tf_op jit(solution)/shard_map/ppermute | solution.py:21
  27.9 20.7 %collective-permute-start.13 = (bf16[4,256,256]{2,1,0:T(8,128)(2,1)S(1)}, bf16[4,256,256]{2,1,0:T(8,128)(2,1)S(1)}, u32[]{:S(2)}, u32[]{:S(2)}) collective-permute-start(bf16[4,256,256]{2,1,0:T(8,128)(2,1)S(1)} %pad_maximum_fusion.1.p0), channel_id=1, source_target_pairs={{0,192},{8,200},{16,208},{24,216},{32,224},{40,232},{48,240},{56,2... | collective-permute-start | bytes 1572872 | tf_op jit(solution)/shard_map/ppermute | solution.py:21
  30.4 19.5 %collective-permute-start.14 = (bf16[4,256,256]{2,1,0:T(8,128)(2,1)S(1)}, bf16[4,256,256]{2,1,0:T(8,128)(2,1)S(1)}, u32[]{:S(2)}, u32[]{:S(2)}) collective-permute-start(bf16[4,256,256]{2,1,0:T(8,128)(2,1)S(1)} %pad_maximum_fusion.1.p0), channel_id=1, source_target_pairs={{0,128},{8,136},{16,144},{24,152},{32,160},{40,168},{48,176},{56,1... | collective-permute-start | bytes 1572872 | tf_op jit(solution)/shard_map/ppermute | solution.py:21
  33.5 7.8 %collective-permute-start.3 = (bf16[256,256]{1,0:T(8,128)(2,1)S(1)}, bf16[256,256]{1,0:T(8,128)(2,1)S(1)}, u32[]{:S(2)}, u32[]{:S(2)}) collective-permute-start(bf16[256,256]{1,0:T(8,128)(2,1)S(1)} %get-tuple-element.19), channel_id=1, source_target_pairs={{0,32},{8,40},{16,48},{24,56},{32,0},{40,8},{48,16},{56,24},{64,96... | collective-permute-start | bytes 393224 | tf_op jit(solution)/shard_map/ppermute | solution.py:21
  41.3 5.7 %collective-permute-start.2 = (bf16[256,256]{1,0:T(8,128)(2,1)S(1)}, bf16[256,256]{1,0:T(8,128)(2,1)S(1)}, u32[]{:S(2)}, u32[]{:S(2)}) collective-permute-start(bf16[256,256]{1,0:T(8,128)(2,1)S(1)} %get-tuple-element.19), channel_id=1, source_target_pairs={{0,48},{8,56},{16,0},{24,8},{32,16},{40,24},{48,32},{56,40},{64,11... | collective-permute-start | bytes 393224 | tf_op jit(solution)/shard_map/ppermute | solution.py:21
  47.0 9.5 %collective-permute-start.15 = (bf16[4,256,256]{2,1,0:T(8,128)(2,1)S(1)}, bf16[4,256,256]{2,1,0:T(8,128)(2,1)}, u32[]{:S(2)}, u32[]{:S(2)}) collective-permute-start(bf16[4,256,256]{2,1,0:T(8,128)(2,1)S(1)} %pad_maximum_fusion.1.p0), channel_id=1, source_target_pairs={{0,64},{8,72},{16,80},{24,88},{32,96},{40,104},{48,112},{56,120},{... | collective-permute-start | bytes 1572872 | tf_op jit(solution)/shard_map/ppermute | solution.py:21
  48.6 21.1 %collective-permute-start.5 = (bf16[4,256,256]{2,1,0:T(8,128)(2,1)S(1)}, bf16[4,256,256]{2,1,0:T(8,128)(2,1)S(1)}, u32[]{:S(2)}, u32[]{:S(2)}) collective-permute-start(bf16[4,256,256]{2,1,0:T(8,128)(2,1)S(1)} %pad_maximum_fusion.p0), channel_id=1, source_target_pairs={{0,192},{8,200},{16,208},{24,216},{32,224},{40,232},{48,240},{56,2... | collective-permute-start | bytes 1572872 | tf_op jit(solution)/shard_map/ppermute | solution.py:21
  50.0 20.1 %collective-permute-start.6 = (bf16[4,256,256]{2,1,0:T(8,128)(2,1)S(1)}, bf16[4,256,256]{2,1,0:T(8,128)(2,1)S(1)}, u32[]{:S(2)}, u32[]{:S(2)}) collective-permute-start(bf16[4,256,256]{2,1,0:T(8,128)(2,1)S(1)} %pad_maximum_fusion.p0), channel_id=1, source_target_pairs={{0,128},{8,136},{16,144},{24,152},{32,160},{40,168},{48,176},{56,1... | collective-permute-start | bytes 1572872 | tf_op jit(solution)/shard_map/ppermute | solution.py:21
  56.5 21.8 %collective-permute-start.7 = (bf16[4,256,256]{2,1,0:T(8,128)(2,1)S(1)}, bf16[4,256,256]{2,1,0:T(8,128)(2,1)S(1)}, u32[]{:S(2)}, u32[]{:S(2)}) collective-permute-start(bf16[4,256,256]{2,1,0:T(8,128)(2,1)S(1)} %pad_maximum_fusion.p0), channel_id=1, source_target_pairs={{0,64},{8,72},{16,80},{24,88},{32,96},{40,104},{48,112},{56,120},{... | collective-permute-start | bytes 1572872 | tf_op jit(solution)/shard_map/ppermute | solution.py:21
  66.7 38.8 %collective-permute-start.17 = (bf16[1536,256]{1,0:T(8,128)(2,1)S(1)}, bf16[1536,256]{1,0:T(8,128)(2,1)S(1)}, u32[]{:S(2)}, u32[]{:S(2)}) collective-permute-start(bf16[1536,256]{1,0:T(8,128)(2,1)S(1)} %shard_map.47.rest_0_), channel_id=1, source_target_pairs={{0,3},{1,0},{2,1},{3,2},{4,7},{5,4},{6,5},{7,6},{8,11},{9,8},{10,9... | collective-permute-start | bytes 2359304 | tf_op jit(solution)/shard_map/ppermute | solution.py:29
  69.7 41.1 %collective-permute-start.19 = (bf16[1536,256]{1,0:T(8,128)(2,1)S(1)}, bf16[1536,256]{1,0:T(8,128)(2,1)S(1)}, u32[]{:S(2)}, u32[]{:S(2)}) collective-permute-start(bf16[1536,256]{1,0:T(8,128)(2,1)S(1)} %shard_map.47.rest_0_), channel_id=1, source_target_pairs={{0,2},{1,3},{2,0},{3,1},{4,6},{5,7},{6,4},{7,5},{8,10},{9,11},{10,... | collective-permute-start | bytes 2359304 | tf_op jit(solution)/shard_map/ppermute | solution.py:29
  70.0 40.7 %collective-permute-start.21 = (bf16[1536,256]{1,0:T(8,128)(2,1)S(1)}, bf16[1536,256]{1,0:T(8,128)(2,1)S(1)}, u32[]{:S(2)}, u32[]{:S(2)}) collective-permute-start(bf16[1536,256]{1,0:T(8,128)(2,1)S(1)} %shard_map.47.rest_0_), channel_id=1, source_target_pairs={{0,1},{1,2},{2,3},{3,0},{4,5},{5,6},{6,7},{7,4},{8,9},{9,10},{10,1... | collective-permute-start | bytes 2359304 | tf_op jit(solution)/shard_map/ppermute | solution.py:29
  78.3 45.1 %collective-permute-start.16 = (bf16[1536,256]{1,0:T(8,128)(2,1)S(1)}, bf16[1536,256]{1,0:T(8,128)(2,1)S(1)}, u32[]{:S(2)}, u32[]{:S(2)}) collective-permute-start(bf16[1536,256]{1,0:T(8,128)(2,1)S(1)} %shard_map.47.rest_0_), channel_id=1, source_target_pairs={{0,8},{8,0},{16,24},{24,16},{32,40},{40,32},{48,56},{56,48},{64,72... | collective-permute-start | bytes 2359304 | tf_op jit(solution)/shard_map/ppermute | solution.py:21
  104.1 19.3 %collective-permute-start.8 = (bf16[256,1536]{1,0:T(8,128)(2,1)S(1)}, bf16[256,1536]{1,0:T(8,128)(2,1)S(1)}, u32[]{:S(2)}, u32[]{:S(2)}) collective-permute-start(bf16[256,1536]{1,0:T(8,128)(2,1)S(1)} %shard_map.46.left0), channel_id=1, source_target_pairs={{0,4},{1,5},{2,6},{3,7},{4,0},{5,1},{6,2},{7,3},{8,12},{9,13},{10,... | collective-permute-start | bytes 2359304 | tf_op jit(solution)/shard_map/ppermute | solution.py:29
  105.5 17.9 %collective-permute-start.18 = (bf16[1536,256]{1,0:T(8,128)(2,1)S(1)}, bf16[1536,256]{1,0:T(8,128)(2,1)S(1)}, u32[]{:S(2)}, u32[]{:S(2)}) collective-permute-start(bf16[1536,256]{1,0:T(8,128)(2,1)S(1)} %collective-permute-done.17.rest_2_), channel_id=1, source_target_pairs={{0,8},{8,0},{16,24},{24,16},{32,40},{40,32},{48,56},{56,48},{64,72... | collective-permute-start | bytes 2359304 | tf_op jit(solution)/shard_map/ppermute | solution.py:21
  110.7 12.7 %collective-permute-start.20 = (bf16[1536,256]{1,0:T(8,128)(2,1)S(1)}, bf16[1536,256]{1,0:T(8,128)(2,1)S(1)}, u32[]{:S(2)}, u32[]{:S(2)}) collective-permute-start(bf16[1536,256]{1,0:T(8,128)(2,1)S(1)} %collective-permute-done.19.rest_4_), channel_id=1, source_target_pairs={{0,8},{8,0},{16,24},{24,16},{32,40},{40,32},{48,56},{56,48},{64,72... | collective-permute-start | bytes 2359304 | tf_op jit(solution)/shard_map/ppermute | solution.py:21
  110.7 12.7 %copy-start = (bf16[1536,256]{1,0:T(8,128)(2,1)}, bf16[1536,256]{1,0:T(8,128)(2,1)S(1)}, u32[]{:S(2)}) copy-start(bf16[1536,256]{1,0:T(8,128)(2,1)S(1)} %collective-permute-done.21.rest_6_) | copy-start | bytes 2359300
  110.7 12.7 %collective-permute-start.22 = (bf16[1536,256]{1,0:T(8,128)(2,1)S(1)}, bf16[1536,256]{1,0:T(8,128)(2,1)S(1)}, u32[]{:S(2)}, u32[]{:S(2)}) collective-permute-start(bf16[1536,256]{1,0:T(8,128)(2,1)S(1)} %collective-permute-done.21.rest_6_), channel_id=1, source_target_pairs={{0,8},{8,0},{16,24},{24,16},{32,40},{40,32},{48,56},{56,48},{64,72... | collective-permute-start | bytes 2359304 | tf_op jit(solution)/shard_map/ppermute | solution.py:21
  123.4 0.9 copy-start.1
  124.3 0.9 copy-start.2
  146.1 14.5 %collective-permute-start.25 = (f16[528,512]{1,0:T(8,128)(2,1)S(1)}, f16[528,512]{1,0:T(8,128)(2,1)S(1)}, u32[]{:S(2)}, u32[]{:S(2)}) collective-permute-start(f16[528,512]{1,0:T(8,128)(2,1)S(1)} %get-tuple-element.9), channel_id=1, source_target_pairs={{0,192},{8,200},{16,208},{24,216},{32,224},{40,232},{48,240},{56,2... | collective-permute-start | bytes 1622024 | tf_op jit(solution)/shard_map/ppermute | solution.py:21
  149.1 14.5 %collective-permute-start.24 = (f16[528,512]{1,0:T(8,128)(2,1)S(1)}, f16[528,512]{1,0:T(8,128)(2,1)S(1)}, u32[]{:S(2)}, u32[]{:S(2)}) collective-permute-start(f16[528,512]{1,0:T(8,128)(2,1)S(1)} %get-tuple-element.8), channel_id=1, source_target_pairs={{0,128},{8,136},{16,144},{24,152},{32,160},{40,168},{48,176},{56,1... | collective-permute-start | bytes 1622024 | tf_op jit(solution)/shard_map/ppermute | solution.py:21
  150.3 26.2 %collective-permute-start.23 = (f16[528,512]{1,0:T(8,128)(2,1)S(1)}, f16[528,512]{1,0:T(8,128)(2,1)S(1)}, u32[]{:S(2)}, u32[]{:S(2)}) collective-permute-start(f16[528,512]{1,0:T(8,128)(2,1)S(1)} %get-tuple-element.7), channel_id=1, source_target_pairs={{0,64},{8,72},{16,80},{24,88},{32,96},{40,104},{48,112},{56,120},{... | collective-permute-start | bytes 1622024 | tf_op jit(solution)/shard_map/ppermute | solution.py:21
  180.7 5.9 %collective-permute-start.28 = (f16[144,512]{1,0:T(8,128)(2,1)S(1)}, f16[144,512]{1,0:T(8,128)(2,1)S(1)}, u32[]{:S(2)}, u32[]{:S(2)}) collective-permute-start(f16[144,512]{1,0:T(8,128)(2,1)S(1)} %concatenate.35), channel_id=1, source_target_pairs={{0,48},{8,56},{16,0},{24,8},{32,16},{40,24},{48,32},{56,40},{64,11... | collective-permute-start | bytes 442376 | tf_op jit(solution)/shard_map/ppermute | solution.py:21
  183.0 15.9 %collective-permute-start.27 = (f16[144,512]{1,0:T(8,128)(2,1)S(1)}, f16[144,512]{1,0:T(8,128)(2,1)S(1)}, u32[]{:S(2)}, u32[]{:S(2)}) collective-permute-start(f16[144,512]{1,0:T(8,128)(2,1)S(1)} %concatenate.34), channel_id=1, source_target_pairs={{0,32},{8,40},{16,48},{24,56},{32,0},{40,8},{48,16},{56,24},{64,96... | collective-permute-start | bytes 442376 | tf_op jit(solution)/shard_map/ppermute | solution.py:21
  185.4 14.6 %collective-permute-start.26 = (f16[144,512]{1,0:T(8,128)(2,1)S(1)}, f16[144,512]{1,0:T(8,128)(2,1)S(1)}, u32[]{:S(2)}, u32[]{:S(2)}) collective-permute-start(f16[144,512]{1,0:T(8,128)(2,1)S(1)} %concatenate.33), channel_id=1, source_target_pairs={{0,16},{8,24},{16,32},{24,40},{32,48},{40,56},{48,0},{56,8},{64,80... | collective-permute-start | bytes 442376 | tf_op jit(solution)/shard_map/ppermute | solution.py:21
  201.3 29.5 %collective-permute-start.29 = (f32[128,512]{1,0:T(8,128)S(1)}, f32[128,512]{1,0:T(8,128)S(1)}, u32[]{:S(2)}, u32[]{:S(2)}) collective-permute-start(f32[128,512]{1,0:T(8,128)S(1)} %fusion.8), channel_id=1, source_target_pairs={{0,0},{1,33},{2,66},{3,99},{4,132},{5,165},{6,198},{7,231},{8,16},... | collective-permute-start | bytes 786440 | tf_op jit(solution)/shard_map/ppermute | solution.py:60

commit v2 on v0

v2 whole, which is shorter than its diff:
```python
import functools

import jax
import jax.numpy as jnp
from jax import lax
from jax.experimental import pallas as pl
from jax.experimental.pallas import tpu as pltpu
from jax.sharding import PartitionSpec as P

NX, NZ, NC, NL, NY = 4, 4, 2, 2, 4
VMEM = 26 << 20
BIAS = 14.0
PAD = 16


def seq_perm(value, move):
    pairs = []
    for i in range(NX * NZ * NC):
        x, zh, c = move(i // (NZ * NC), i // NC % NZ, i % NC)
        pairs.append((i, ((x % NX) * NZ + zh % NZ) * NC + c % NC))
    return lax.ppermute(value, "seq", pairs)


def basis_perm(value, move):
    pairs = []
    for j in range(NL * NY):
        zl, y = move(j // NY, j % NY)
        pairs.append((j, (zl % NL) * NY + y % NY))
    return lax.ppermute(value, "basis", pairs)


def swap_core(value):
    return seq_perm(value, lambda x, zh, c: (x, zh, c + 1))


def from_x(value, d):
    return seq_perm(value, lambda x, zh, c: (x - d, zh, c))


def from_zh(value, d):
    return seq_perm(value, lambda x, zh, c: (x, zh - d, c))


def from_y(value, d):
    return basis_perm(value, lambda zl, y: (zl, y - d))


def swap_zl(value):
    return basis_perm(value, lambda zl, y: (zl + 1, y))


def all_x(copies):
    groups = [[(x * NZ + zh) * NC + c for x in range(NX)] for zh in range(NZ) for c in range(NC)]
    return lax.all_to_all(copies, "seq", 0, 0, axis_index_groups=groups, tiled=True)


def to_owner(value, k):
    pairs = []
    for i in range(NX * NZ * NC):
        for j in range(NL * NY):
            xt, zt, c, zl, y = i // (NZ * NC), i // NC % NZ, i % NC, j // NY, j % NY
            x, zh, core = xt - xt % 2 + y // 2, 2 * (y % 2) + c, (xt % 2) ^ (y // 2)
            seq, basis = (x * NZ + zh) * NC + core, zl * NY + (y + zt + k) % NY
            pairs.append((i * NL * NY + j, seq * NL * NY + basis))
    return lax.ppermute(value, ("seq", "basis"), pairs)


def power_of(top):
    return jnp.clip(jnp.ceil(jnp.log2(top)), -100.0, 130.0)


def grow(sent):
    wide = sent.astype(jnp.float32)
    return wide[:-PAD] * jnp.exp2(wide[-PAD : 1 - PAD] - BIAS)


def product_kernel(seq_len, places, left0, left1, left2, *rest):
    grads, (out, left, right, left_sem, right_sem) = rest[:8], rest[8:]
    rows = left1.shape[0]
    width = grads[0].shape[1]
    seqs = left.shape[1] // seq_len
    lefts = [
        pltpu.make_async_copy(ref, left.at[pl.ds(at * rows, ref.shape[0]), :], left_sem.at[i])
        for i, (at, ref) in enumerate(((0, left0), (2, left1), (3, left2)))
    ]
    rights = [pltpu.make_async_copy(ref, right.at[g], right_sem.at[g]) for g, ref in enumerate(grads)]
    for copy in lefts + rights:
        copy.start()
    for copy in lefts:
        copy.wait()

    top = jnp.zeros((8, width), jnp.float32)
    for g in range(8):
        rights[g].wait()
        row = pl.multiple_of(places[NX + g // 2] * rows, rows)
        column = pl.multiple_of((places[NX + NZ] ^ (g % 2)) * width, width)
        shift = seqs // 2 if g % 2 else 0

        def one(d, top):
            at = pl.multiple_of(places[d] * rows, rows)
            total = None
            for s in range(seqs):
                from_token = (s + shift) % seqs * seq_len
                product = jnp.dot(
                    left[pl.ds(at, rows), s * seq_len : (s + 1) * seq_len],
                    right[g, from_token : from_token + seq_len, :],
                    preferred_element_type=jnp.float32,
                )
                total = product * product if total is None else total + product * product
            out[d, pl.ds(row, rows), pl.ds(column, width)] = total
            return jnp.maximum(top, jnp.max(total.reshape(rows // 8, 8, width), axis=0))

        for d in range(NX):
            top = one(d, top)
    power = power_of(jnp.max(jnp.max(top, axis=0, keepdims=True), axis=1, keepdims=True))
    for d in range(1, NX):
        out[d, : NZ * rows, :] = out[d, : NZ * rows, :] * jnp.exp2(BIAS - power)
        out[d, NZ * rows :, :] = jnp.broadcast_to(power, (PAD, 2 * width))
    out[0, NZ * rows :, :] = jnp.full((PAD, 2 * width), BIAS)


def products(places, left, grads, seq_len):
    half, tokens = left[0].shape
    width = grads[0].shape[1]
    return pl.pallas_call(
        functools.partial(product_kernel, seq_len),
        out_shape=jax.ShapeDtypeStruct((NX, 2 * half + PAD, 2 * width), jnp.float32),
        in_specs=[pl.BlockSpec(memory_space=pltpu.SMEM)] + [pl.BlockSpec(memory_space=pl.ANY)] * 11,
        out_specs=pl.BlockSpec(memory_space=pltpu.VMEM),
        scratch_shapes=[
            pltpu.VMEM((2 * half, tokens), jnp.bfloat16),
            pltpu.VMEM((8, tokens, width), jnp.bfloat16),
            pltpu.SemaphoreType.DMA((3,)),
            pltpu.SemaphoreType.DMA((8,)),
        ],
        compiler_params=pltpu.CompilerParams(vmem_limit_bytes=VMEM),
        cost_estimate=pl.CostEstimate(
            flops=32 * half * tokens * width, bytes_accessed=20 * tokens * width, transcendentals=0
        ),
    )(places, *left, *grads)


def stack_zh(shard, zh):
    column = jnp.stack([shard] + [from_zh(shard, d) for d in range(1, NZ)])
    twice = jnp.concatenate([column, column])
    column = lax.dynamic_slice_in_dim(twice, (NZ - zh) % NZ, NZ, 0)
    return column.reshape(NZ * shard.shape[0], shard.shape[1])


def per_device(activations, gradients, act_basis, grad_basis):
    seq_count, seq_len, width = activations.shape
    seq, basis = lax.axis_index("seq"), lax.axis_index("basis")
    x, zh, core = seq // (NZ * NC), seq // NC % NZ, seq % NC
    zl, y = basis // NY, basis % NY
    act = activations.reshape(seq_count * seq_len, width)
    grad = gradients.reshape(seq_count * seq_len, width)

    half = act_basis.shape[0] // 2

    def rows_at(which):
        start = which * half
        return [lax.dynamic_slice_in_dim(shard, start, half, 0).T for shard in (grad_basis, act_basis)]

    kept = jnp.concatenate(rows_at(core), 1)
    got = swap_core(jnp.concatenate(rows_at(1 - core), 1))
    pair = jnp.where(core == 0, jnp.concatenate([kept, got]), jnp.concatenate([got, kept]))
    grad_column = stack_zh(pair[:, :half], zh)
    copies = jnp.broadcast_to(grad_column[None], (NX,) + grad_column.shape)
    act_pair, copies, grad, act = lax.optimization_barrier((pair[:, half:], copies, grad, act))
    grad_rows = all_x(copies).reshape(-1, half)
    grad_sib = swap_core(grad)
    act_column = stack_zh(act_pair, zh)
    act_sib = swap_core(act)
    act_column, grad_rows, grad_sib, act_sib = lax.optimization_barrier(
        (act_column, grad_rows, grad_sib, act_sib)
    )
    act_columns = [act_column] + [from_x(act_column, d) for d in range(1, NX)]

    def rotate_grad(block):
        return jnp.dot(block, grad_rows, preferred_element_type=jnp.float32).astype(jnp.bfloat16)

    rotated_grad = jnp.concatenate([rotate_grad(grad), rotate_grad(grad_sib)])
    act_columns, fenced = lax.optimization_barrier((act_columns, rotated_grad))
    act_rows = jnp.zeros((NX,) + act_column.shape, act_column.dtype)
    for d in range(NX):
        act_rows = lax.dynamic_update_slice(act_rows, act_columns[d][None], ((x + d) % NX, 0, 0))
    act_rows = act_rows.reshape(-1, half)

    def rotate_act(block):
        total = lax.dot_general(
            act_rows, block, (((0,), (1,)), ((), ())), preferred_element_type=jnp.float32
        )
        return total.astype(jnp.bfloat16)

    rotated_act = jnp.concatenate([rotate_act(act), rotate_act(act_sib)], 1)

    far = [from_y(rotated_grad, d) for d in range(1, NY)]
    pieces = [swap_zl(rotated_act[: half // 2]), swap_zl(rotated_act[half // 2 :])]
    far, near, pieces = lax.optimization_barrier((far, rotated_act, pieces))
    both = []
    for block in [fenced] + far:
        both += [block, swap_core(block)]

    steps = jnp.arange(4)
    target = (x + steps) % NX
    rows_of = 2 * ((target // 2) ^ zl) + ((target % 2) ^ (y // 2))
    places = jnp.concatenate([rows_of, (steps - zh) % NZ, core[None]]).astype(jnp.int32)
    terms = products(places, [near] + pieces, both, seq_len)

    total = terms[0, :-PAD]
    for d in range(1, NX):
        total = total + grow(from_x(terms[d].astype(jnp.float16), -d))
    rows = total.shape[0] // NZ
    power = power_of(jnp.max(total))
    final = None
    for k in range(NZ):
        block = total[k * rows : (k + 1) * rows] * jnp.exp2(BIAS - power)
        sent = jnp.concatenate([block, jnp.full((PAD, block.shape[1]), power)]).astype(jnp.float16)
        part = grow(to_owner(sent, k))
        final = part if final is None else final + part
    all_seqs = seq_count * NX * NZ * NC
    return final / jnp.float32(all_seqs * seq_len)


def solution(mesh):
    placed = (P("seq", None, None), P("seq", None, None), P("basis", "seq"), P("basis", "seq"))
    return jax.shard_map(
        per_device, mesh=mesh, in_specs=placed, out_specs=P("seq", "basis"), check_vma=False
    )
```

time: 400 us -> 203 us (0.51)
  waiting for transfers between devices: 314 us -> 102 us
  starting transfers between devices: 0.3 us -> 60.2 us
  other arithmetic: 32.6 us -> 3.53 us
  matrix products: 38.5 us -> 18.6 us
  between operations: 13.1 us -> 1.25 us
  Pallas kernels: 0 us -> 9.37 us
  local copies, waits for them, and re-layouts: 1.22 us -> 7.47 us
    all_gather x3 -> x0, waiting for transfers between devices: 193 us -> none  [the longest x1 70.8 us: per_device(): lax.all_gather(act_basis, 'seq', axis=1, tiled=True)]
    reduce_scatter x1 -> x0, waiting for transfers between devices: 120 us -> none  [per_device(): summed = lax.psum_scatter(terms, 'seq', scatter_dimension=0, tiled=True)]
    ppermute x0 -> x28, waiting for transfers between devices: none -> 81.6 us  [the longest x19 53.1 us: seq_perm(): return lax.ppermute(value, 'seq', pairs)]
    ppermute x0 -> x28, starting transfers between devices: none -> 55.6 us  [the longest x19 35.3 us: seq_perm(): return lax.ppermute(value, 'seq', pairs)]
    add x3 -> x0, other arithmetic: 31 us -> none  [per_pair(): return running + jnp.sum(product * product, axis=0)]
    all_to_all x0 -> x1, waiting for transfers between devices: none -> 20.8 us  [all_x(): lax.all_to_all(copies, 'seq', 0, 0, axis_index_groups=groups, tiled=True)]
    dot_general x5 -> x4, matrix products: 38.5 us -> 18.6 us  [the longest x2 9.5 us: rotate_act(): lax.dot_general(act_rows, block, (((0,), (1,)), ((), ())), preferred_elem...]
    pallas_call x0 -> x1, Pallas kernels: none -> 9.37 us  [products(): pl.pallas_call(functools.partial(product_kernel, seq_len), out_shape=jax....]
  transfers between devices with their start and end apart: 4 -> 29, of which waited for: 4 -> 18; matrix products, arithmetic and copies ran while one was open for 4% -> 11% of each run, Pallas kernels for 0% -> 0%
where the time goes in v2:
time: 203 us
  waiting for transfers between devices  102 us (50%)
  starting transfers between devices  60.2 us (30%)
  matrix products  18.6 us (9%)
  Pallas kernels  9.37 us (5%)
  local copies, waits for them, and re-layouts  7.47 us (4%)
  other arithmetic  3.53 us (2%)
    ppermute x19, waiting for transfers between devices, seq_perm(): return lax.ppermute(value, 'seq', pairs)  53.1 us
    ppermute x19, starting transfers between devices, seq_perm(): return lax.ppermute(value, 'seq', pairs)  35.3 us
    all_to_all x1, waiting for transfers between devices, all_x(): lax.all_to_all(copies, 'seq', 0, 0, axis_index_groups=groups, tiled=True)  20.8 us
    ppermute x4, waiting for transfers between devices, to_owner(): return lax.ppermute(value, ('seq', 'basis'), pairs)  20 us
    ppermute x4, starting transfers between devices, to_owner(): return lax.ppermute(value, ('seq', 'basis'), pairs)  14.7 us
    dot_general x2, matrix products, rotate_act(): lax.dot_general(act_rows, block, (((0,), (1,)), ((), ())), preferred_elem...  9.5 us
    pallas_call x1, Pallas kernels, products(): pl.pallas_call(functools.partial(product_kernel, seq_len), out_shape=jax....  9.37 us
    dot_general x2, matrix products, rotate_grad(): jnp.dot(block, grad_rows, preferred_element_type=jnp.float32)  9.15 us
  transfers between devices with their start and end apart: 29, of which 18 were waited for; matrix products, arithmetic and copies ran while one was open for 11% of the time, Pallas kernels for 0%

profile of v2, /device:TPU:1, one launch (start us, length us, event | category | flops | bytes accessed | tf_op | source)
XLA Modules:
  0.0 202.9 jit_solution(10825103737447133361)
XLA Ops:
  0.0 1.0 constant_dynamic-slice_fusion.4
  1.0 0.1 copy.12
  1.1 0.1 copy.11
  1.2 3.3 %collective-permute-start = (bf16[128,512]{1,0:T(8,128)(2,1)S(1)}, bf16[128,512]{1,0:T(8,128)(2,1)S(1)}, u32[]{:S(2)}, u32[]{:S(2)}) collective-permute-start(bf16[128,512]{1,0:T(8,128)(2,1)S(1)} %pad_maximum_fusion.2), channel_id=1, source_target_pairs={{0,8},{8,0},{16,24},{24,16},{32,40},{40,32},{48,56},{56,48},{64,72... | collective-permute-start | bytes 393224 | tf_op jit(solution)/shard_map/ppermute | solution.py:21
  4.8 0.7 collective-permute-done
  5.6 4.4 %collective-permute-start.1 = (bf16[256,256]{1,0:T(8,128)(2,1)S(1)}, bf16[256,256]{1,0:T(8,128)(2,1)S(1)}, u32[]{:S(2)}, u32[]{:S(2)}) collective-permute-start(bf16[256,256]{1,0:T(8,128)(2,1)S(1)} %get-tuple-element.54), channel_id=1, source_target_pairs={{0,48},{8,56},{16,0},{24,8},{32,16},{40,24},{48,32},{56,40},{64,11... | collective-permute-start | bytes 393224 | tf_op jit(solution)/shard_map/ppermute | solution.py:21
  10.0 1.0 collective-permute-start.2
  11.0 2.3 %collective-permute-start.3 = (bf16[256,256]{1,0:T(8,128)(2,1)S(1)}, bf16[256,256]{1,0:T(8,128)(2,1)S(1)}, u32[]{:S(2)}, u32[]{:S(2)}) collective-permute-start(bf16[256,256]{1,0:T(8,128)(2,1)S(1)} %get-tuple-element.54), channel_id=1, source_target_pairs={{0,16},{8,24},{16,32},{24,40},{32,48},{40,56},{48,0},{56,8},{64,80... | collective-permute-start | bytes 393224 | tf_op jit(solution)/shard_map/ppermute | solution.py:21
  13.2 1.3 collective-permute-done.1
  14.6 6.7 %collective-permute-done.2 = bf16[256,256]{1,0:T(8,128)(2,1)S(1)} collective-permute-done((bf16[256,256]{1,0:T(8,128)(2,1)S(1)}, bf16[256,256]{1,0:T(8,128)(2,1)S(1)}, u32[]{:S(2)}, u32[]{:S(2)}) %collective-permute-start.2) | collective-permute-done | bytes 131104 | tf_op jit(solution)/shard_map/ppermute | solution.py:21
  21.6 1.5 broadcast_in_dim.31
  23.0 2.8 %collective-permute-start.7 = (bf16[768,4096]{1,0:T(8,128)(2,1)}, bf16[768,4096]{1,0:T(8,128)(2,1)}, u32[]{:S(2)}, u32[]{:S(2)}) collective-permute-start(bf16[768,4096]{1,0:T(8,128)(2,1)} %bitcast.10), channel_id=1, source_target_pairs={{0,8},{8,0},{16,24},{24,16},{32,40},{40,32},{48,56},{56,48},{64,72... | collective-permute-start | bytes 18874376 | tf_op jit(solution)/shard_map/ppermute | solution.py:21
  25.9 3.0 %collective-permute-start.4 = (bf16[256,256]{1,0:T(8,128)(2,1)S(1)}, bf16[256,256]{1,0:T(8,128)(2,1)S(1)}, u32[]{:S(2)}, u32[]{:S(2)}) collective-permute-start(bf16[256,256]{1,0:T(8,128)(2,1)S(1)} %get-tuple-element.25), channel_id=1, source_target_pairs={{0,48},{8,56},{16,0},{24,8},{32,16},{40,24},{48,32},{56,40},{64,11... | collective-permute-start | bytes 393224 | tf_op jit(solution)/shard_map/ppermute | solution.py:21
  28.9 1.8 collective-permute-start.5
  30.7 2.0 collective-permute-start.6
  32.8 4.6 %all-to-all-start = ((bf16[4,1024,256]{2,1,0:T(8,128)(2,1)}), bf16[4,1024,256]{2,1,0:T(8,128)(2,1)S(1)}, u32[]{:S(2)}, u32[]{:S(2)}) async-start(bf16[4,1024,256]{2,1,0:T(8,128)(2,1)} %broadcast_in_dim.31), calls=%async_computation | async-start | bytes 4194304 | tf_op jit(solution)/shard_map/all_to_all | solution.py:54
  37.4 2.9 %collective-permute-done.6 = bf16[256,256]{1,0:T(8,128)(2,1)S(1)} collective-permute-done((bf16[256,256]{1,0:T(8,128)(2,1)S(1)}, bf16[256,256]{1,0:T(8,128)(2,1)S(1)}, u32[]{:S(2)}, u32[]{:S(2)}) %collective-permute-start.6) | collective-permute-done | bytes 131104 | tf_op jit(solution)/shard_map/ppermute | solution.py:21
  40.4 0.9 constant_dynamic-slice_fusion
  41.3 20.8 %all-to-all-done = bf16[4,1024,256]{2,1,0:T(8,128)(2,1)S(1)} async-done(((bf16[4,1024,256]{2,1,0:T(8,128)(2,1)}), bf16[4,1024,256]{2,1,0:T(8,128)(2,1)S(1)}, u32[]{:S(2)}, u32[]{:S(2)}) %all-to-all-start) | async-done | bytes 2097184 | tf_op jit(solution)/shard_map/all_to_all | solution.py:54
  62.1 0.9 collective-permute-start.12
  63.0 1.2 collective-permute-start.13
  64.2 4.6 %convolution_convert_fusion.3 = bf16[768,256]{1,0:T(8,128)(2,1)S(1)} fusion(bf16[768,4096]{1,0:T(8,128)(2,1)} %bitcast.10, bf16[4096,256]{1,0:T(8,128)(2,1)S(1)} %bitcast.72), kind=kOutput, calls=%fused_computation.3 | convolution fusion | flops 1610809344 | bytes 8781824 | tf_op jit(solution)/shard_map/dot_general | solution.py:180
  68.7 4.6 %convolution_convert_fusion.2 = bf16[768,256]{1,0:T(8,128)(2,1)S(1)} fusion(bf16[768,4096]{1,0:T(8,128)(2,1)} %collective-permute-done.7, bf16[4096,256]{1,0:T(8,128)(2,1)S(1)} %bitcast.73), kind=kOutput, calls=%fused_computation.2 | convolution fusion | flops 1610809344 | bytes 8781824 | tf_op jit(solution)/shard_map/dot_general | solution.py:180
  73.4 3.0 %collective-permute-start.9 = (bf16[1536,256]{1,0:T(8,128)(2,1)S(1)}, bf16[1536,256]{1,0:T(8,128)(2,1)S(1)}, u32[]{:S(2)}, u32[]{:S(2)}) collective-permute-start(bf16[1536,256]{1,0:T(8,128)(2,1)S(1)} %pad_maximum_fusion.1.rest_0_), channel_id=1, source_target_pairs={{0,3},{1,0},{2,1},{3,2},{4,7},{5,4},{6,5},{7,6},{8,11},{9,8},{10,9... | collective-permute-start | bytes 2359304 | tf_op jit(solution)/shard_map/ppermute | solution.py:29
  76.4 0.4 collective-permute-start.10
  76.7 0.7 collective-permute-start.11
  77.4 12.3 %collective-permute-done.14 = bf16[1024,256]{1,0:T(8,128)(2,1)S(1)} collective-permute-done((bf16[1024,256]{1,0:T(8,128)(2,1)}, bf16[1024,256]{1,0:T(8,128)(2,1)S(1)}, u32[]{:S(2)}, u32[]{:S(2)}) %collective-permute-start.14) | collective-permute-done | bytes 524320 | tf_op jit(solution)/shard_map/ppermute | solution.py:21
  89.8 0.1 broadcast_in_dim.32
  89.9 1.1 bitcast_dynamic-update-slice_fusion.3
  91.1 4.8 %convolution_convert_fusion.1 = bf16[256,768]{1,0:T(8,128)(2,1)S(1)} fusion(bf16[4096,256]{1,0:T(8,128)(2,1)S(1)} %bitcast.69, bf16[768,4096]{1,0:T(8,128)(2,1)} %bitcast.11), kind=kOutput, calls=%fused_computation.1 | convolution fusion | flops 1610809344 | bytes 8781824 | tf_op jit(solution)/shard_map/dot_general | solution.py:190
  95.9 4.8 %convolution_convert_fusion = bf16[256,768]{1,0:T(8,128)(2,1)S(1)} fusion(bf16[4096,256]{1,0:T(8,128)(2,1)S(1)} %bitcast.70, bf16[768,4096]{1,0:T(8,128)(2,1)} %collective-permute-done.8), kind=kOutput, calls=%fused_computation | convolution fusion | flops 1610809344 | bytes 8781824 | tf_op jit(solution)/shard_map/dot_general | solution.py:190
  100.7 1.3 collective-permute-start.15
  102.0 0.2 collective-permute-start.16
  102.3 8.6 %collective-permute-start.17 = (bf16[1536,256]{1,0:T(8,128)(2,1)S(1)}, bf16[1536,256]{1,0:T(8,128)(2,1)}, u32[]{:S(2)}, u32[]{:S(2)}) collective-permute-start(bf16[1536,256]{1,0:T(8,128)(2,1)S(1)} %pad_maximum_fusion.1.rest_0_), channel_id=1, source_target_pairs={{0,8},{8,0},{16,24},{24,16},{32,40},{40,32},{48,56},{56,48},{64,72... | collective-permute-start | bytes 2359304 | tf_op jit(solution)/shard_map/ppermute | solution.py:21
  111.0 3.3 %collective-permute-done.11.rest_6_ = bf16[1536,256]{1,0:T(8,128)(2,1)} collective-permute-done((bf16[1536,256]{1,0:T(8,128)(2,1)S(1)}, bf16[1536,256]{1,0:T(8,128)(2,1)}, u32[]{:S(2)}, u32[]{:S(2)}) %collective-permute-start.11) | collective-permute-done | bytes 786464 | tf_op jit(solution)/shard_map/ppermute | solution.py:29
  114.3 5.1 %collective-permute-done.16.left2 = bf16[128,1536]{1,0:T(8,128)(2,1)S(1)} collective-permute-done((bf16[128,1536]{1,0:T(8,128)(2,1)S(1)}, bf16[128,1536]{1,0:T(8,128)(2,1)S(1)}, u32[]{:S(2)}, u32[]{:S(2)}) %collective-permute-start.16) | collective-permute-done | bytes 393248 | tf_op jit(solution)/shard_map/ppermute | solution.py:29
  119.4 0.8 copy-done
  120.2 1.3 collective-permute-start.18
  121.5 0.5 collective-permute-start.20
  122.2 1.4 collective-permute-done.18.rest_3_
  123.6 2.2 %collective-permute-done.19.rest_5_ = bf16[1536,256]{1,0:T(8,128)(2,1)} collective-permute-done((bf16[1536,256]{1,0:T(8,128)(2,1)S(1)}, bf16[1536,256]{1,0:T(8,128)(2,1)}, u32[]{:S(2)}, u32[]{:S(2)}) %collective-permute-start.19) | collective-permute-done | bytes 786464 | tf_op jit(solution)/shard_map/ppermute | solution.py:21
  125.8 0.2 collective-permute-done.20.rest_7_
  126.0 1.0 copy-done.1
  127.0 9.4 %shard_map.46 = f32[4,528,512]{2,1,0:T(8,128)S(1)} custom-call(s32[9]{0:T(128)S(1)} %pad_add_fusion.places, bf16[256,1536]{1,0:T(8,128)(2,1)S(1)} %pad_maximum_fusion.left0, bf16[128,1536]{1,0:T(8,128)(2,1)S(1)} %collective-permute-done.15.left1, bf16[128,1536]{1,0:T(8,128)(2,1)S(1)} %copy-done.1, bf16[1536,256]{1,0:T(8,128)(2,1)S(1)} %pad_maximum_fusion.1.rest_0_, ...), custom_call_target="tpu_custom_call" | custom-call | flops 3221225472 | bytes 7864320 | tf_op jit(solution)/shard_map/pallas_call | solution.py:125
  136.4 0.6 convert.23
  137.0 0.3 slice_bitcast_fusion.3
  137.4 1.3 collective-permute-start.22
  138.7 0.8 collective-permute-start.21
  139.5 11.4 %collective-permute-done.23 = f16[528,512]{1,0:T(8,128)(2,1)S(1)} collective-permute-done((f16[528,512]{1,0:T(8,128)(2,1)S(1)}, f16[528,512]{1,0:T(8,128)(2,1)S(1)}, u32[]{:S(2)}, u32[]{:S(2)}) %collective-permute-start.23) | collective-permute-done | bytes 540704 | tf_op jit(solution)/shard_map/ppermute | solution.py:21
  150.9 0.1 convert_element_type.58
  151.1 1.5 collective-permute-done.22
  152.6 0.1 convert_element_type.56
  152.7 12.1 %collective-permute-done.21 = f16[528,512]{1,0:T(8,128)(2,1)S(1)} collective-permute-done((f16[528,512]{1,0:T(8,128)(2,1)S(1)}, f16[528,512]{1,0:T(8,128)(2,1)S(1)}, u32[]{:S(2)}, u32[]{:S(2)}) %collective-permute-start.21) | collective-permute-done | bytes 540704 | tf_op jit(solution)/shard_map/ppermute | solution.py:21
  164.8 0.1 convert_element_type.54
  165.0 1.1 fusion.31
  166.8 0.1 fusion.12
  167.0 4.7 %collective-permute-start.27 = (f16[144,512]{1,0:T(8,128)(2,1)S(1)}, f16[144,512]{1,0:T(8,128)(2,1)S(1)}, u32[]{:S(2)}, u32[]{:S(2)}) collective-permute-start(f16[144,512]{1,0:T(8,128)(2,1)S(1)} %concatenate.53), channel_id=1, source_target_pairs={{0,3},{1,32},{2,73},{3,106},{4,7},{5,36},{6,77},{7,110},{8,19},{9,... | collective-permute-start | bytes 442376 | tf_op jit(solution)/shard_map/ppermute | solution.py:65
  171.7 2.1 %collective-permute-start.26 = (f16[144,512]{1,0:T(8,128)(2,1)S(1)}, f16[144,512]{1,0:T(8,128)(2,1)S(1)}, u32[]{:S(2)}, u32[]{:S(2)}) collective-permute-start(f16[144,512]{1,0:T(8,128)(2,1)S(1)} %concatenate.52), channel_id=1, source_target_pairs={{0,2},{1,35},{2,72},{3,105},{4,6},{5,39},{6,76},{7,109},{8,18},{9,... | collective-permute-start | bytes 442376 | tf_op jit(solution)/shard_map/ppermute | solution.py:65
  173.8 3.8 %collective-permute-start.25 = (f16[144,512]{1,0:T(8,128)(2,1)S(1)}, f16[144,512]{1,0:T(8,128)(2,1)S(1)}, u32[]{:S(2)}, u32[]{:S(2)}) collective-permute-start(f16[144,512]{1,0:T(8,128)(2,1)S(1)} %concatenate.51), channel_id=1, source_target_pairs={{0,1},{1,34},{2,75},{3,104},{4,5},{5,38},{6,79},{7,108},{8,17},{9,... | collective-permute-start | bytes 442376 | tf_op jit(solution)/shard_map/ppermute | solution.py:65
  177.7 4.1 %collective-permute-start.24 = (f16[144,512]{1,0:T(8,128)(2,1)S(1)}, f16[144,512]{1,0:T(8,128)(2,1)S(1)}, u32[]{:S(2)}, u32[]{:S(2)}) collective-permute-start(f16[144,512]{1,0:T(8,128)(2,1)S(1)} %concatenate.50), channel_id=1, source_target_pairs={{0,0},{1,33},{2,74},{3,107},{4,4},{5,37},{6,78},{7,111},{8,16},{9,... | collective-permute-start | bytes 442376 | tf_op jit(solution)/shard_map/ppermute | solution.py:65
  181.9 3.3 %collective-permute-done.26 = f16[144,512]{1,0:T(8,128)(2,1)S(1)} collective-permute-done((f16[144,512]{1,0:T(8,128)(2,1)S(1)}, f16[144,512]{1,0:T(8,128)(2,1)S(1)}, u32[]{:S(2)}, u32[]{:S(2)}) %collective-permute-start.26) | collective-permute-done | bytes 147488 | tf_op jit(solution)/shard_map/ppermute | solution.py:65
  185.3 11.2 %collective-permute-done.25 = f16[144,512]{1,0:T(8,128)(2,1)S(1)} collective-permute-done((f16[144,512]{1,0:T(8,128)(2,1)S(1)}, f16[144,512]{1,0:T(8,128)(2,1)S(1)}, u32[]{:S(2)}, u32[]{:S(2)}) %collective-permute-start.25) | collective-permute-done | bytes 147488 | tf_op jit(solution)/shard_map/ppermute | solution.py:65
  196.5 5.5 %collective-permute-done.24 = f16[144,512]{1,0:T(8,128)(2,1)S(1)} collective-permute-done((f16[144,512]{1,0:T(8,128)(2,1)S(1)}, f16[144,512]{1,0:T(8,128)(2,1)S(1)}, u32[]{:S(2)}, u32[]{:S(2)}) %collective-permute-start.24) | collective-permute-done | bytes 147488 | tf_op jit(solution)/shard_map/ppermute | solution.py:65
  202.0 0.8 fusion.6
  (63 shorter events, 1.4 us)
Async XLA Ops:
  1.2 4.3 %collective-permute-start = (bf16[128,512]{1,0:T(8,128)(2,1)S(1)}, bf16[128,512]{1,0:T(8,128)(2,1)S(1)}, u32[]{:S(2)}, u32[]{:S(2)}) collective-permute-start(bf16[128,512]{1,0:T(8,128)(2,1)S(1)} %pad_maximum_fusion.2), channel_id=1, source_target_pairs={{0,8},{8,0},{16,24},{24,16},{32,40},{40,32},{48,56},{56,48},{64,72... | collective-permute-start | bytes 393224 | tf_op jit(solution)/shard_map/ppermute | solution.py:21
  5.6 9.0 %collective-permute-start.1 = (bf16[256,256]{1,0:T(8,128)(2,1)S(1)}, bf16[256,256]{1,0:T(8,128)(2,1)S(1)}, u32[]{:S(2)}, u32[]{:S(2)}) collective-permute-start(bf16[256,256]{1,0:T(8,128)(2,1)S(1)} %get-tuple-element.54), channel_id=1, source_target_pairs={{0,48},{8,56},{16,0},{24,8},{32,16},{40,24},{48,32},{56,40},{64,11... | collective-permute-start | bytes 393224 | tf_op jit(solution)/shard_map/ppermute | solution.py:21
  10.0 11.4 %collective-permute-start.2 = (bf16[256,256]{1,0:T(8,128)(2,1)S(1)}, bf16[256,256]{1,0:T(8,128)(2,1)S(1)}, u32[]{:S(2)}, u32[]{:S(2)}) collective-permute-start(bf16[256,256]{1,0:T(8,128)(2,1)S(1)} %get-tuple-element.54), channel_id=1, source_target_pairs={{0,32},{8,40},{16,48},{24,56},{32,0},{40,8},{48,16},{56,24},{64,96... | collective-permute-start | bytes 393224 | tf_op jit(solution)/shard_map/ppermute | solution.py:21
  11.0 10.5 %collective-permute-start.3 = (bf16[256,256]{1,0:T(8,128)(2,1)S(1)}, bf16[256,256]{1,0:T(8,128)(2,1)S(1)}, u32[]{:S(2)}, u32[]{:S(2)}) collective-permute-start(bf16[256,256]{1,0:T(8,128)(2,1)S(1)} %get-tuple-element.54), channel_id=1, source_target_pairs={{0,16},{8,24},{16,32},{24,40},{32,48},{40,56},{48,0},{56,8},{64,80... | collective-permute-start | bytes 393224 | tf_op jit(solution)/shard_map/ppermute | solution.py:21
  23.0 39.0 %collective-permute-start.7 = (bf16[768,4096]{1,0:T(8,128)(2,1)}, bf16[768,4096]{1,0:T(8,128)(2,1)}, u32[]{:S(2)}, u32[]{:S(2)}) collective-permute-start(bf16[768,4096]{1,0:T(8,128)(2,1)} %bitcast.10), channel_id=1, source_target_pairs={{0,8},{8,0},{16,24},{24,16},{32,40},{40,32},{48,56},{56,48},{64,72... | collective-permute-start | bytes 18874376 | tf_op jit(solution)/shard_map/ppermute | solution.py:21
  25.9 36.2 %collective-permute-start.8 = (bf16[768,4096]{1,0:T(8,128)(2,1)}, bf16[768,4096]{1,0:T(8,128)(2,1)}, u32[]{:S(2)}, u32[]{:S(2)}) collective-permute-start(bf16[768,4096]{1,0:T(8,128)(2,1)} %bitcast.11), channel_id=1, source_target_pairs={{0,8},{8,0},{16,24},{24,16},{32,40},{40,32},{48,56},{56,48},{64,72... | collective-permute-start | bytes 18874376 | tf_op jit(solution)/shard_map/ppermute | solution.py:21
  25.9 11.5 %collective-permute-start.4 = (bf16[256,256]{1,0:T(8,128)(2,1)S(1)}, bf16[256,256]{1,0:T(8,128)(2,1)S(1)}, u32[]{:S(2)}, u32[]{:S(2)}) collective-permute-start(bf16[256,256]{1,0:T(8,128)(2,1)S(1)} %get-tuple-element.25), channel_id=1, source_target_pairs={{0,48},{8,56},{16,0},{24,8},{32,16},{40,24},{48,32},{56,40},{64,11... | collective-permute-start | bytes 393224 | tf_op jit(solution)/shard_map/ppermute | solution.py:21
  28.9 8.5 %collective-permute-start.5 = (bf16[256,256]{1,0:T(8,128)(2,1)S(1)}, bf16[256,256]{1,0:T(8,128)(2,1)S(1)}, u32[]{:S(2)}, u32[]{:S(2)}) collective-permute-start(bf16[256,256]{1,0:T(8,128)(2,1)S(1)} %get-tuple-element.25), channel_id=1, source_target_pairs={{0,32},{8,40},{16,48},{24,56},{32,0},{40,8},{48,16},{56,24},{64,96... | collective-permute-start | bytes 393224 | tf_op jit(solution)/shard_map/ppermute | solution.py:21
  30.7 9.6 %collective-permute-start.6 = (bf16[256,256]{1,0:T(8,128)(2,1)S(1)}, bf16[256,256]{1,0:T(8,128)(2,1)S(1)}, u32[]{:S(2)}, u32[]{:S(2)}) collective-permute-start(bf16[256,256]{1,0:T(8,128)(2,1)S(1)} %get-tuple-element.25), channel_id=1, source_target_pairs={{0,16},{8,24},{16,32},{24,40},{32,48},{40,56},{48,0},{56,8},{64,80... | collective-permute-start | bytes 393224 | tf_op jit(solution)/shard_map/ppermute | solution.py:21
  32.8 29.3 %all-to-all-start = ((bf16[4,1024,256]{2,1,0:T(8,128)(2,1)}), bf16[4,1024,256]{2,1,0:T(8,128)(2,1)S(1)}, u32[]{:S(2)}, u32[]{:S(2)}) async-start(bf16[4,1024,256]{2,1,0:T(8,128)(2,1)} %broadcast_in_dim.31), calls=%async_computation | async-start | bytes 4194304 | tf_op jit(solution)/shard_map/all_to_all | solution.py:54
  62.1 14.6 %collective-permute-start.12 = (bf16[1024,256]{1,0:T(8,128)(2,1)}, bf16[1024,256]{1,0:T(8,128)(2,1)S(1)}, u32[]{:S(2)}, u32[]{:S(2)}) collective-permute-start(bf16[1024,256]{1,0:T(8,128)(2,1)} %bitcast.16), channel_id=1, source_target_pairs={{0,192},{8,200},{16,208},{24,216},{32,224},{40,232},{48,240},{56,2... | collective-permute-start | bytes 1572872 | tf_op jit(solution)/shard_map/ppermute | solution.py:21
  63.0 14.4 %collective-permute-start.13 = (bf16[1024,256]{1,0:T(8,128)(2,1)}, bf16[1024,256]{1,0:T(8,128)(2,1)S(1)}, u32[]{:S(2)}, u32[]{:S(2)}) collective-permute-start(bf16[1024,256]{1,0:T(8,128)(2,1)} %bitcast.16), channel_id=1, source_target_pairs={{0,128},{8,136},{16,144},{24,152},{32,160},{40,168},{48,176},{56,1... | collective-permute-start | bytes 1572872 | tf_op jit(solution)/shard_map/ppermute | solution.py:21
  64.2 25.6 %collective-permute-start.14 = (bf16[1024,256]{1,0:T(8,128)(2,1)}, bf16[1024,256]{1,0:T(8,128)(2,1)S(1)}, u32[]{:S(2)}, u32[]{:S(2)}) collective-permute-start(bf16[1024,256]{1,0:T(8,128)(2,1)} %bitcast.16), channel_id=1, source_target_pairs={{0,64},{8,72},{16,80},{24,88},{32,96},{40,104},{48,112},{56,120},{... | collective-permute-start | bytes 1572872 | tf_op jit(solution)/shard_map/ppermute | solution.py:21
  73.4 29.0 %collective-permute-start.9 = (bf16[1536,256]{1,0:T(8,128)(2,1)S(1)}, bf16[1536,256]{1,0:T(8,128)(2,1)S(1)}, u32[]{:S(2)}, u32[]{:S(2)}) collective-permute-start(bf16[1536,256]{1,0:T(8,128)(2,1)S(1)} %pad_maximum_fusion.1.rest_0_), channel_id=1, source_target_pairs={{0,3},{1,0},{2,1},{3,2},{4,7},{5,4},{6,5},{7,6},{8,11},{9,8},{10,9... | collective-permute-start | bytes 2359304 | tf_op jit(solution)/shard_map/ppermute | solution.py:29
  76.4 34.6 %collective-permute-start.10 = (bf16[1536,256]{1,0:T(8,128)(2,1)S(1)}, bf16[1536,256]{1,0:T(8,128)(2,1)S(1)}, u32[]{:S(2)}, u32[]{:S(2)}) collective-permute-start(bf16[1536,256]{1,0:T(8,128)(2,1)S(1)} %pad_maximum_fusion.1.rest_0_), channel_id=1, source_target_pairs={{0,2},{1,3},{2,0},{3,1},{4,6},{5,7},{6,4},{7,5},{8,10},{9,11},{10,... | collective-permute-start | bytes 2359304 | tf_op jit(solution)/shard_map/ppermute | solution.py:29
  76.7 37.6 %collective-permute-start.11 = (bf16[1536,256]{1,0:T(8,128)(2,1)S(1)}, bf16[1536,256]{1,0:T(8,128)(2,1)}, u32[]{:S(2)}, u32[]{:S(2)}) collective-permute-start(bf16[1536,256]{1,0:T(8,128)(2,1)S(1)} %pad_maximum_fusion.1.rest_0_), channel_id=1, source_target_pairs={{0,1},{1,2},{2,3},{3,0},{4,5},{5,6},{6,7},{7,4},{8,9},{9,10},{10,1... | collective-permute-start | bytes 2359304 | tf_op jit(solution)/shard_map/ppermute | solution.py:29
  100.7 13.6 %collective-permute-start.15 = (bf16[128,1536]{1,0:T(8,128)(2,1)S(1)}, bf16[128,1536]{1,0:T(8,128)(2,1)S(1)}, u32[]{:S(2)}, u32[]{:S(2)}) collective-permute-start(bf16[128,1536]{1,0:T(8,128)(2,1)S(1)} %get-tuple-element.53), channel_id=1, source_target_pairs={{0,4},{1,5},{2,6},{3,7},{4,0},{5,1},{6,2},{7,3},{8,12},{9,13},{10,... | collective-permute-start | bytes 1179656 | tf_op jit(solution)/shard_map/ppermute | solution.py:29
  102.0 17.4 %collective-permute-start.16 = (bf16[128,1536]{1,0:T(8,128)(2,1)S(1)}, bf16[128,1536]{1,0:T(8,128)(2,1)S(1)}, u32[]{:S(2)}, u32[]{:S(2)}) collective-permute-start(bf16[128,1536]{1,0:T(8,128)(2,1)S(1)} %get-tuple-element.52), channel_id=1, source_target_pairs={{0,4},{1,5},{2,6},{3,7},{4,0},{5,1},{6,2},{7,3},{8,12},{9,13},{10,... | collective-permute-start | bytes 1179656 | tf_op jit(solution)/shard_map/ppermute | solution.py:29
  102.3 19.8 %collective-permute-start.17 = (bf16[1536,256]{1,0:T(8,128)(2,1)S(1)}, bf16[1536,256]{1,0:T(8,128)(2,1)}, u32[]{:S(2)}, u32[]{:S(2)}) collective-permute-start(bf16[1536,256]{1,0:T(8,128)(2,1)S(1)} %pad_maximum_fusion.1.rest_0_), channel_id=1, source_target_pairs={{0,8},{8,0},{16,24},{24,16},{32,40},{40,32},{48,56},{56,48},{64,72... | collective-permute-start | bytes 2359304 | tf_op jit(solution)/shard_map/ppermute | solution.py:21
  119.4 0.8 copy-start
  120.2 3.4 %collective-permute-start.18 = (bf16[1536,256]{1,0:T(8,128)(2,1)S(1)}, bf16[1536,256]{1,0:T(8,128)(2,1)}, u32[]{:S(2)}, u32[]{:S(2)}) collective-permute-start(bf16[1536,256]{1,0:T(8,128)(2,1)S(1)} %collective-permute-done.9.rest_2_), channel_id=1, source_target_pairs={{0,8},{8,0},{16,24},{24,16},{32,40},{40,32},{48,56},{56,48},{64,72... | collective-permute-start | bytes 2359304 | tf_op jit(solution)/shard_map/ppermute | solution.py:21
  121.5 4.3 %collective-permute-start.19 = (bf16[1536,256]{1,0:T(8,128)(2,1)S(1)}, bf16[1536,256]{1,0:T(8,128)(2,1)}, u32[]{:S(2)}, u32[]{:S(2)}) collective-permute-start(bf16[1536,256]{1,0:T(8,128)(2,1)S(1)} %collective-permute-done.10.rest_4_), channel_id=1, source_target_pairs={{0,8},{8,0},{16,24},{24,16},{32,40},{40,32},{48,56},{56,48},{64,72... | collective-permute-start | bytes 2359304 | tf_op jit(solution)/shard_map/ppermute | solution.py:21
  121.5 4.5 %collective-permute-start.20 = (bf16[1536,256]{1,0:T(8,128)(2,1)}, bf16[1536,256]{1,0:T(8,128)(2,1)}, u32[]{:S(2)}, u32[]{:S(2)}) collective-permute-start(bf16[1536,256]{1,0:T(8,128)(2,1)} %collective-permute-done.11.rest_6_), channel_id=1, source_target_pairs={{0,8},{8,0},{16,24},{24,16},{32,40},{40,32},{48,56},{56,48},{64,72... | collective-permute-start | bytes 2359304 | tf_op jit(solution)/shard_map/ppermute | solution.py:21
  126.0 1.0 copy-start.1
  137.3 13.6 %collective-permute-start.23 = (f16[528,512]{1,0:T(8,128)(2,1)S(1)}, f16[528,512]{1,0:T(8,128)(2,1)S(1)}, u32[]{:S(2)}, u32[]{:S(2)}) collective-permute-start(f16[528,512]{1,0:T(8,128)(2,1)S(1)} %get-tuple-element.46), channel_id=1, source_target_pairs={{0,192},{8,200},{16,208},{24,216},{32,224},{40,232},{48,240},{56,2... | collective-permute-start | bytes 1622024 | tf_op jit(solution)/shard_map/ppermute | solution.py:21
  137.4 15.1 %collective-permute-start.22 = (f16[528,512]{1,0:T(8,128)(2,1)S(1)}, f16[528,512]{1,0:T(8,128)(2,1)S(1)}, u32[]{:S(2)}, u32[]{:S(2)}) collective-permute-start(f16[528,512]{1,0:T(8,128)(2,1)S(1)} %get-tuple-element.47), channel_id=1, source_target_pairs={{0,128},{8,136},{16,144},{24,152},{32,160},{40,168},{48,176},{56,1... | collective-permute-start | bytes 1622024 | tf_op jit(solution)/shard_map/ppermute | solution.py:21
  138.7 26.1 %collective-permute-start.21 = (f16[528,512]{1,0:T(8,128)(2,1)S(1)}, f16[528,512]{1,0:T(8,128)(2,1)S(1)}, u32[]{:S(2)}, u32[]{:S(2)}) collective-permute-start(f16[528,512]{1,0:T(8,128)(2,1)S(1)} %get-tuple-element.45), channel_id=1, source_target_pairs={{0,64},{8,72},{16,80},{24,88},{32,96},{40,104},{48,112},{56,120},{... | collective-permute-start | bytes 1622024 | tf_op jit(solution)/shard_map/ppermute | solution.py:21
  167.0 14.8 %collective-permute-start.27 = (f16[144,512]{1,0:T(8,128)(2,1)S(1)}, f16[144,512]{1,0:T(8,128)(2,1)S(1)}, u32[]{:S(2)}, u32[]{:S(2)}) collective-permute-start(f16[144,512]{1,0:T(8,128)(2,1)S(1)} %concatenate.53), channel_id=1, source_target_pairs={{0,3},{1,32},{2,73},{3,106},{4,7},{5,36},{6,77},{7,110},{8,19},{9,... | collective-permute-start | bytes 442376 | tf_op jit(solution)/shard_map/ppermute | solution.py:65
  171.7 13.5 %collective-permute-start.26 = (f16[144,512]{1,0:T(8,128)(2,1)S(1)}, f16[144,512]{1,0:T(8,128)(2,1)S(1)}, u32[]{:S(2)}, u32[]{:S(2)}) collective-permute-start(f16[144,512]{1,0:T(8,128)(2,1)S(1)} %concatenate.52), channel_id=1, source_target_pairs={{0,2},{1,35},{2,72},{3,105},{4,6},{5,39},{6,76},{7,109},{8,18},{9,... | collective-permute-start | bytes 442376 | tf_op jit(solution)/shard_map/ppermute | solution.py:65
  173.8 22.6 %collective-permute-start.25 = (f16[144,512]{1,0:T(8,128)(2,1)S(1)}, f16[144,512]{1,0:T(8,128)(2,1)S(1)}, u32[]{:S(2)}, u32[]{:S(2)}) collective-permute-start(f16[144,512]{1,0:T(8,128)(2,1)S(1)} %concatenate.51), channel_id=1, source_target_pairs={{0,1},{1,34},{2,75},{3,104},{4,5},{5,38},{6,79},{7,108},{8,17},{9,... | collective-permute-start | bytes 442376 | tf_op jit(solution)/shard_map/ppermute | solution.py:65
  177.7 24.3 %collective-permute-start.24 = (f16[144,512]{1,0:T(8,128)(2,1)S(1)}, f16[144,512]{1,0:T(8,128)(2,1)S(1)}, u32[]{:S(2)}, u32[]{:S(2)}) collective-permute-start(f16[144,512]{1,0:T(8,128)(2,1)S(1)} %concatenate.50), channel_id=1, source_target_pairs={{0,0},{1,33},{2,74},{3,107},{4,4},{5,37},{6,78},{7,111},{8,16},{9,... | collective-permute-start | bytes 442376 | tf_op jit(solution)/shard_map/ppermute | solution.py:65
